TPU v7x, 256 devices: a whole 4x4x8 slice. The times are simulated.
256 devices in a mesh: role: 64 (over x, y, z_hi, core), tp: 4 (over z_lo).
Axes of the slice: x: 4, y: 4, z: 8 (z_hi: 2, z_lo: 4; z = z_hi * 4 + z_lo), core: 2. Of those that a mesh axis runs over, the one named last changes fastest.
Arguments:
- prompt_q: bfloat16 [64, 64, 8192], P('role', None, 'tp'), may hold values from -60 to 60
- prompt_kv: bfloat16 [64, 2, 192, 1024], P('role', None, None, 'tp'), may hold values from -4.2 to 4.2
- prefix_length: int32 [64], P('role'), may hold values from 1 to 128
- decode_q: bfloat16 [64, 128, 2, 8192], P('role', 'tp'), may hold values from -60 to 60
- decode_kv: bfloat16 [64, 128, 2, 16, 1024], P('role', 'tp'), may hold values from -9 to 9
- fresh_kv: bfloat16 [64, 128, 2, 2, 1024], P('role', 'tp'), may hold values from -16 to 16
- source_prompt: int32 [64, 128, 1], P('role', 'tp'), may hold values from 0 to 63; in each aligned block of 32 rows (0 to 31, 32 to 63, ..., all dimensions but the last counted through in order) at most 2 rows name the same one
- cache_length: int32 [64, 128], P('role', 'tp'), may hold values from 2 to 16
Outputs:
- prompt_out: bfloat16 [64, 64, 8192], P('role', None, 'tp')
- decode_out: bfloat16 [64, 128, 2, 8192], P('role', 'tp')
Inputs may be any that keep to these rules, and one draw needn't show every extreme that they name: `source_prompt`: among the 32 sequences of one device, no prompt is named more than 2 times.
All inputs are finite; a program needn't handle non-finite values.
Results may differ from a plain program's by a relative error of at most 0.0045.
Values may be sent and summed in bfloat16 or wider, within the bound.
A program may use at most 128 MiB of HBM per device.

v0:
```python
import math

import jax
import jax.numpy as jnp
from jax import lax
from jax.sharding import PartitionSpec as P

HEADS = 64
KVH = 8
HD = 128


NEGATIVE = -1e30


def softmax_terms(scores, usable):
    masked = jnp.where(usable, scores, NEGATIVE)
    highest = jnp.max(masked, axis=-1)
    terms = jnp.where(usable, jnp.exp(masked - highest[..., None]), 0.0)
    return (highest, jnp.sum(terms, axis=-1), terms.astype(jnp.bfloat16))


def prefill_attention(prompt_q, prompt_kv, prefix_rows, score_scale):
    stretch_rows = prompt_q.shape[1]
    key_rows = prompt_kv.shape[2]
    before = key_rows - stretch_rows
    kv_local = prompt_kv.shape[3] // HD
    per_kv = HEADS // KVH
    queries = prompt_q[0].reshape(stretch_rows, kv_local, per_kv, HD)
    prompt_keys = prompt_kv[0, 0].reshape(key_rows, kv_local, HD)
    prompt_values = prompt_kv[0, 1].reshape(key_rows, kv_local, HD)
    scores = (
        jnp.einsum("icgd,tcd->icgt", queries, prompt_keys, preferred_element_type=jnp.float32)
        * score_scale
    )
    positions = jnp.arange(key_rows, dtype=jnp.int32)
    own_row = jnp.arange(stretch_rows, dtype=jnp.int32)[:, None]
    usable = (positions[None, :] < prefix_rows) | (positions[None, :] >= before) & (
        positions[None, :] - before <= own_row
    )
    highest, weight_sum, weights = softmax_terms(scores, usable[:, None, None, :])
    weighted = jnp.einsum(
        "icgt,tcd->icgd", weights, prompt_values, preferred_element_type=jnp.float32
    )
    result = (weighted / weight_sum[..., None]).astype(jnp.bfloat16)
    return result.reshape(1, stretch_rows, kv_local * per_kv * HD)


def remote_every(asked_rows, prompt_keys, prompt_values, prefix_rows, before, score_scale):
    scores = (
        jnp.einsum("rcgd,tcd->rcgt", asked_rows, prompt_keys, preferred_element_type=jnp.float32)
        * score_scale
    )
    positions = jnp.arange(prompt_keys.shape[0], dtype=jnp.int32)
    usable = (positions < prefix_rows) | (positions >= before)
    highest, weight_sum, weights = softmax_terms(scores, usable)
    weighted = jnp.einsum(
        "rcgt,tcd->rcgd", weights, prompt_values, preferred_element_type=jnp.float32
    )
    return (weighted / weight_sum[..., None], highest, weight_sum)


def shards(
    prompt_q, prompt_kv, prefix_length, decode_q, decode_kv, fresh_kv, source_prompt, cache_length
):
    score_scale = 1.0 / math.sqrt(HD)
    per_kv = HEADS // KVH
    role_count = lax.axis_size("role")
    tp_count = lax.axis_size("tp")
    seq_count = decode_q.shape[1]
    step_count = decode_q.shape[2]
    feature_width = decode_q.shape[3]
    capacity = max(2, 2 * seq_count // role_count)
    slot_count = role_count * capacity
    targets = source_prompt[0, :, 0]
    prompt_hits = (targets[:, None] == jnp.arange(role_count, dtype=jnp.int32)[None, :]).astype(
        jnp.int32
    )
    bucket_rank = jnp.cumsum(prompt_hits, axis=0) - 1
    slot_index = targets * capacity + jnp.sum(bucket_rank * prompt_hits, axis=1)
    placement = (slot_index[:, None] == jnp.arange(slot_count, dtype=jnp.int32)[None, :]).astype(
        jnp.bfloat16
    )
    flat_queries = decode_q[0].reshape(seq_count, step_count * feature_width)
    outgoing = jnp.einsum(
        "sm,sq->mq", placement, flat_queries, preferred_element_type=jnp.float32
    ).astype(jnp.bfloat16)
    outgoing = outgoing.reshape(
        role_count, capacity, step_count, tp_count, feature_width // tp_count
    )
    incoming = lax.all_to_all(
        lax.all_to_all(outgoing, "role", split_axis=0, concat_axis=0, tiled=True),
        "tp",
        split_axis=3,
        concat_axis=3,
        tiled=True,
    )
    prefix_rows = prefix_length[0]
    prompt_out = prefill_attention(prompt_q, prompt_kv, prefix_rows, score_scale)
    key_rows = prompt_kv.shape[2]
    before = key_rows - prompt_q.shape[1]
    kv_local = prompt_kv.shape[3] // HD
    prompt_keys = prompt_kv[0, 0].reshape(key_rows, kv_local, HD)
    prompt_values = prompt_kv[0, 1].reshape(key_rows, kv_local, HD)
    asked_count = role_count * capacity * step_count * tp_count
    block_rows = 128
    asked_rows = incoming.reshape(asked_count // block_rows, block_rows, kv_local, per_kv, HD)

    def answer(row_block):
        return remote_every(row_block, prompt_keys, prompt_values, prefix_rows, before, score_scale)

    remote_out, remote_max, remote_sum = lax.map(answer, asked_rows)
    head_local = kv_local * per_kv
    remote_out = remote_out.reshape(role_count, capacity, step_count, tp_count, head_local * HD)
    remote_max = remote_max.reshape(role_count, capacity, step_count, tp_count, head_local)
    remote_sum = remote_sum.reshape(role_count, capacity, step_count, tp_count, head_local)
    back_out, back_max, back_sum = (
        lax.all_to_all(
            lax.all_to_all(remote_out, "role", split_axis=0, concat_axis=0, tiled=True),
            "tp",
            split_axis=3,
            concat_axis=3,
            tiled=True,
        ),
        lax.all_to_all(
            lax.all_to_all(remote_max, "role", split_axis=0, concat_axis=0, tiled=True),
            "tp",
            split_axis=3,
            concat_axis=3,
            tiled=True,
        ),
        lax.all_to_all(
            lax.all_to_all(remote_sum, "role", split_axis=0, concat_axis=0, tiled=True),
            "tp",
            split_axis=3,
            concat_axis=3,
            tiled=True,
        ),
    )
    own_out = jnp.take(back_out.reshape(slot_count, step_count, feature_width), slot_index, axis=0)
    own_out = own_out.reshape(seq_count, step_count, KVH, per_kv, HD)
    own_max = jnp.take(back_max.reshape(slot_count, step_count, HEADS), slot_index, axis=0).reshape(
        seq_count, step_count, KVH, per_kv
    )
    own_sum = jnp.take(back_sum.reshape(slot_count, step_count, HEADS), slot_index, axis=0).reshape(
        seq_count, step_count, KVH, per_kv
    )
    cache_rows = decode_kv.shape[3]
    queries = decode_q[0].reshape(seq_count, step_count, KVH, per_kv, HD)
    cache_keys = decode_kv[0, :, 0].reshape(seq_count, cache_rows, KVH, HD)
    cache_values = decode_kv[0, :, 1].reshape(seq_count, cache_rows, KVH, HD)
    fresh_keys = fresh_kv[0, :, 0].reshape(seq_count, step_count, KVH, HD)
    fresh_values = fresh_kv[0, :, 1].reshape(seq_count, step_count, KVH, HD)
    cache_scores = (
        jnp.einsum("sxcgd,stcd->sxcgt", queries, cache_keys, preferred_element_type=jnp.float32)
        * score_scale
    )
    fresh_scores = (
        jnp.einsum("sxcgd,stcd->sxcgt", queries, fresh_keys, preferred_element_type=jnp.float32)
        * score_scale
    )
    cache_usable = (jnp.arange(cache_rows, dtype=jnp.int32)[None, :] < cache_length[0][:, None])[
        :, None, None, None, :
    ]
    step_index = jnp.arange(step_count, dtype=jnp.int32)
    fresh_usable = (step_index[None, :] <= step_index[:, None])[None, :, None, None, :]
    local_max = jnp.maximum(
        jnp.max(jnp.where(cache_usable, cache_scores, NEGATIVE), axis=-1),
        jnp.max(jnp.where(fresh_usable, fresh_scores, NEGATIVE), axis=-1),
    )
    cache_terms = jnp.where(cache_usable, jnp.exp(cache_scores - local_max[..., None]), 0.0)
    fresh_terms = jnp.where(fresh_usable, jnp.exp(fresh_scores - local_max[..., None]), 0.0)
    local_sum = jnp.sum(cache_terms, axis=-1) + jnp.sum(fresh_terms, axis=-1)
    local_weighted = jnp.einsum(
        "sxcgt,stcd->sxcgd",
        cache_terms.astype(jnp.bfloat16),
        cache_values,
        preferred_element_type=jnp.float32,
    )
    local_weighted = local_weighted + jnp.einsum(
        "sxcgt,stcd->sxcgd",
        fresh_terms.astype(jnp.bfloat16),
        fresh_values,
        preferred_element_type=jnp.float32,
    )
    local_out = local_weighted / local_sum[..., None]
    joint_peak = jnp.maximum(own_max, local_max)
    remote_share = own_sum * jnp.exp(own_max - joint_peak)
    local_share = local_sum * jnp.exp(local_max - joint_peak)
    merged = (remote_share[..., None] * own_out + local_share[..., None] * local_out) / (
        remote_share + local_share
    )[..., None]
    decode_out = merged.astype(jnp.bfloat16).reshape(1, seq_count, step_count, feature_width)
    return (prompt_out, decode_out)


def solution(mesh):
    return jax.shard_map(
        shards,
        mesh=mesh,
        in_specs=(
            P("role", None, "tp"),
            P("role", None, None, "tp"),
            P("role"),
            P("role", "tp", None, None),
            P("role", "tp", None, None, None),
            P("role", "tp", None, None, None),
            P("role", "tp", None),
            P("role", "tp"),
        ),
        out_specs=(P("role", None, "tp"), P("role", "tp", None, None)),
        check_vma=False,
    )
```

profile of v0, /device:TPU:1, one launch (start us, length us, event | category | flops | bytes accessed | tf_op | source)
XLA Modules:
  0.0 824.3 jit_solution(5406525748283093019)
XLA Ops:
  8.0 7.8 reshape.241
  15.8 6.5 copy.150
  22.3 116.2 %all_to_all.40 = bf16[64,2,2,4,2048]{4,2,1,3,0:T(2,128)(2,1)} all-to-all(bf16[64,2,2,4,2048]{4,2,1,3,0:T(2,128)(2,1)S(1)} %copy.150), channel_id=1, replica_groups=mesh['role'=64,'tp'=4] {'role'}, dimensions={0} | all-to-all | bytes 8388608 | tf_op jit(solution)/shard_map/all_to_all | solution.py:92
  138.5 9.7 %copy.151 = bf16[64,2,2,4,2048]{4,2,1,0,3:T(2,128)(2,1)} copy(bf16[64,2,2,4,2048]{4,2,1,3,0:T(2,128)(2,1)} %all_to_all.40) | data formatting | bytes 8388608 | tf_op jit(solution)/shard_map/all_to_all | solution.py:92
  153.5 92.8 %all-to-all-done.1 = bf16[64,2,2,4,2048]{4,2,1,0,3:T(2,128)(2,1)} async-done(((bf16[64,2,2,4,2048]{4,2,1,0,3:T(2,128)(2,1)}), bf16[64,2,2,4,2048]{4,2,1,0,3:T(2,128)(2,1)}, u32[]{:S(2)}, u32[]{:S(2)}) %all-to-all-start.1) | async-done | bytes 4194336 | tf_op jit(solution)/shard_map/all_to_all | solution.py:91
  246.3 12.1 %copy.152 = bf16[64,2,2,4,2048]{4,3,2,1,0:T(4,128)(2,1)} copy(bf16[64,2,2,4,2048]{4,2,1,0,3:T(2,128)(2,1)} %all-to-all-done.1) | data formatting | bytes 8388608 | tf_op jit(solution)/shard_map/all_to_all | solution.py:91
  258.4 7.7 reshape.242
  266.0 39.0 %while.14 = (s32[]{:T(128)}, f32[8,128,2,8,128]{4,3,2,1,0:T(8,128)}, f32[8,128,2,8]{1,3,2,0:T(8,128)S(1)}, f32[8,128,2,8]{1,3,2,0:T(8,128)S(1)}, s32[]{:T(128)},...) while((s32[]{:T(128)}, ...), condition=%wide.region_7.8_spmd, body=%wide.region_4.7_spmd.sunk | while | flops 205124160 | bytes 9708905 | solution.py:112
  305.0 11.5 %copy.156 = f32[8,128,2,8]{3,2,1,0:T(2,128)S(1)} copy(f32[8,128,2,8]{1,3,2,0:T(8,128)S(1)} %get-tuple-element.47) | data formatting | bytes 131072 | tf_op jit(solution)/shard_map/while | solution.py:112
  318.3 5.3 all-to-all-start.2
  325.9 9.7 %all-to-all-done.2 = f32[64,1,256]{2,1,0:T(1,128)S(1)} async-done(((f32[64,1,256]{2,1,0:T(1,128)}), f32[64,1,256]{2,1,0:T(1,128)S(1)}, u32[]{:S(2)}, u32[]{:S(2)}) %all-to-all-start.2) | async-done | bytes 65568 | tf_op jit(solution)/shard_map/all_to_all | solution.py:133
  342.9 9.4 %all-to-all-done.4 = f32[64,1,256]{2,1,0:T(1,128)S(1)} async-done(((f32[64,1,256]{2,1,0:T(1,128)}), f32[64,1,256]{2,1,0:T(1,128)S(1)}, u32[]{:S(2)}, u32[]{:S(2)}) %all-to-all-start.4) | async-done | bytes 65568 | tf_op jit(solution)/shard_map/all_to_all | solution.py:126
  355.5 9.9 %reshape.249 = f32[64,2,2,4,2048]{4,3,2,1,0:T(4,128)} reshape(f32[8,128,2,8,128]{4,3,2,1,0:T(8,128)} %get-tuple-element.49) | data formatting | bytes 16777216 | tf_op jit(solution)/shard_map/reshape | solution.py:114
  365.5 5.6 all-to-all-start.6
  373.2 102.0 %all-to-all-done.6 = f32[64,2,2,4,2048]{4,3,2,1,0:T(4,128)} async-done(((f32[64,2,2,4,2048]{4,3,2,1,0:T(4,128)}), f32[64,2,2,4,2048]{4,3,2,1,0:T(4,128)}, u32[]{:S(2)}, u32[]{:S(2)}) %all-to-all-start.6) | async-done | bytes 8388640 | tf_op jit(solution)/shard_map/all_to_all | solution.py:119
  475.2 101.5 %all-to-all-start.5 = ((f32[4,1,4096]{2,1,0:T(1,128)}), f32[4,1,4096]{2,1,0:T(1,128)S(1)}, u32[]{:S(2)}, u32[]{:S(2)}) async-start(f32[4,1,4096]{2,1,0:T(1,128)} %reshape.296), calls=%async_computation.5 | async-start | bytes 131072 | tf_op jit(solution)/shard_map/all_to_all | solution.py:125
  576.7 15.4 %copy.173 = f32[64,2,2,4,2048]{4,2,1,0,3:T(2,128)} copy(f32[64,2,2,4,2048]{4,3,2,1,0:T(4,128)} %all-to-all-done.6) | data formatting | bytes 16777216 | tf_op jit(solution)/shard_map/all_to_all | solution.py:119
  592.1 5.8 all-to-all-start.7
  604.3 6.1 select_reduce_fusion
  631.6 148.8 %all-to-all-done.7 = f32[64,2,2,4,2048]{4,2,1,0,3:T(2,128)} async-done(((f32[64,2,2,4,2048]{4,2,1,0,3:T(2,128)}), f32[64,2,2,4,2048]{4,2,1,0,3:T(2,128)}, u32[]{:S(2)}, u32[]{:S(2)}) %all-to-all-start.7) | async-done | bytes 8388640 | tf_op jit(solution)/shard_map/all_to_all | solution.py:118
  780.4 15.4 %copy.174 = f32[64,2,2,4,2048]{4,3,2,1,0:T(4,128)} copy(f32[64,2,2,4,2048]{4,2,1,0,3:T(2,128)} %all-to-all-done.7) | data formatting | bytes 16777216 | tf_op jit(solution)/shard_map/all_to_all | solution.py:118
  795.8 12.6 %reshape.250 = f32[128,2,8192]{2,1,0:T(2,128)} reshape(f32[64,2,2,4,2048]{4,3,2,1,0:T(4,128)} %copy.174) | data formatting | bytes 16777216 | tf_op jit(solution)/shard_map/reshape | solution.py:140
  808.4 6.2 gather_fusion
  817.5 5.3 fusion.21
  (157 shorter events, 99.1 us)
Async XLA Ops:
  148.2 5.1 copy-start.3
  148.2 98.0 %all-to-all-start.1 = ((bf16[64,2,2,4,2048]{4,2,1,0,3:T(2,128)(2,1)}), bf16[64,2,2,4,2048]{4,2,1,0,3:T(2,128)(2,1)}, u32[]{:S(2)}, u32[]{:S(2)}) async-start(bf16[64,2,2,4,2048]{4,2,1,0,3:T(2,128)(2,1)} %copy.151), calls=%async_computation.1 | async-start | bytes 8388608 | tf_op jit(solution)/shard_map/all_to_all | solution.py:91
  318.3 17.3 %all-to-all-start.2 = ((f32[64,1,256]{2,1,0:T(1,128)}), f32[64,1,256]{2,1,0:T(1,128)S(1)}, u32[]{:S(2)}, u32[]{:S(2)}) async-start(f32[64,1,256]{2,1,0:T(1,128)} %reshape.298), calls=%async_computation.2 | async-start | bytes 131072 | tf_op jit(solution)/shard_map/all_to_all | solution.py:133
  335.6 16.6 %all-to-all-start.4 = ((f32[64,1,256]{2,1,0:T(1,128)}), f32[64,1,256]{2,1,0:T(1,128)S(1)}, u32[]{:S(2)}, u32[]{:S(2)}) async-start(f32[64,1,256]{2,1,0:T(1,128)} %reshape.294), calls=%async_computation.4 | async-start | bytes 131072 | tf_op jit(solution)/shard_map/all_to_all | solution.py:126
  352.2 13.2 %all-to-all-start.3 = ((f32[4,1,4096]{2,1,0:T(1,128)}), f32[4,1,4096]{2,1,0:T(1,128)S(1)}, u32[]{:S(2)}, u32[]{:S(2)}) async-start(f32[4,1,4096]{2,1,0:T(1,128)} %reshape.300), calls=%async_computation.3 | async-start | bytes 131072 | tf_op jit(solution)/shard_map/all_to_all | solution.py:132
  365.5 109.7 %all-to-all-start.6 = ((f32[64,2,2,4,2048]{4,3,2,1,0:T(4,128)}), f32[64,2,2,4,2048]{4,3,2,1,0:T(4,128)}, u32[]{:S(2)}, u32[]{:S(2)}) async-start(f32[64,2,2,4,2048]{4,3,2,1,0:T(4,128)} %reshape.249), calls=%async_computation.6 | async-start | bytes 16777216 | tf_op jit(solution)/shard_map/all_to_all | solution.py:119
  475.2 116.9 %all-to-all-start.5 = ((f32[4,1,4096]{2,1,0:T(1,128)}), f32[4,1,4096]{2,1,0:T(1,128)S(1)}, u32[]{:S(2)}, u32[]{:S(2)}) async-start(f32[4,1,4096]{2,1,0:T(1,128)} %reshape.296), calls=%async_computation.5 | async-start | bytes 131072 | tf_op jit(solution)/shard_map/all_to_all | solution.py:125
  592.1 5.8 copy-start
  592.1 188.4 %all-to-all-start.7 = ((f32[64,2,2,4,2048]{4,2,1,0,3:T(2,128)}), f32[64,2,2,4,2048]{4,2,1,0,3:T(2,128)}, u32[]{:S(2)}, u32[]{:S(2)}) async-start(f32[64,2,2,4,2048]{4,2,1,0,3:T(2,128)} %copy.173), calls=%async_computation.7 | async-start | bytes 16777216 | tf_op jit(solution)/shard_map/all_to_all | solution.py:118
  598.7 3.2 copy-start.2
  601.1 0.7 copy-start.7
  602.0 2.4 copy-start.4
  617.9 2.5 copy-start.6
  619.5 2.0 copy-start.5
  814.6 2.9 copy-start.1
where the time goes:
time: 832 us; the launch traced here: 824 us
  waiting for transfers between devices  363 us (44%)
  local copies, waits for them, and re-layouts  164 us (20%)
  starting transfers between devices  131 us (16%)
  blocking collectives  116 us (14%)
  matrix products  31.1 us (4%)
  other arithmetic  17.4 us (2%)
    all_to_all x1, waiting for transfers between devices, shards(): lax.all_to_all(lax.all_to_all(remote_out, 'role', split_axis=0, concat_ax...  149 us
    all_to_all x1, blocking collectives, shards(): lax.all_to_all(outgoing, 'role', split_axis=0, concat_axis=0, tiled=True)  116 us
    all_to_all x1, waiting for transfers between devices, shards(): lax.all_to_all(remote_out, 'role', split_axis=0, concat_axis=0, tiled=True)  102 us
    all_to_all x1, starting transfers between devices, shards(): lax.all_to_all(lax.all_to_all(remote_max, 'role', split_axis=0, concat_ax...  102 us
    all_to_all x1, waiting for transfers between devices, shards(): lax.all_to_all(lax.all_to_all(outgoing, 'role', split_axis=0, concat_axis...  92.8 us
  transfers between devices with their start and end apart: 7, of which 5 were waited for; matrix products, arithmetic and copies ran while one was open for 8% of the time, Pallas kernels for 0%

commit v1 on v0

v1 whole, which is shorter than its diff:
```python
import functools
import math

import jax
import jax.numpy as jnp
from jax import lax
from jax.experimental import pallas as pl
from jax.experimental.pallas import tpu as pltpu
from jax.sharding import PartitionSpec as P

HEADS = 64
KVH = 8
PER_KV = HEADS // KVH
HD = 128
C = 64
PRE = 128
KEYS = PRE + C
LOC = 16
SEQ = 32
STEPS = 2
ROWS = PER_KV * STEPS
NX, NY, NZH, NC, NZL = 4, 4, 2, 2, 4
RING = NZH * NZL
SLOTS = NC * NX * NY
SCALE = 1.0 / math.sqrt(HD)
NEGATIVE = -1e30
LOCAL_KEYS = KVH * (LOC + STEPS)

F32 = jnp.float32
BF16 = jnp.bfloat16
VMEM = pltpu.VMEM
MIB = 1024 * 1024


def position():
    role = lax.axis_index("role")
    z_lo = lax.axis_index("tp")
    core = lax.rem(role, NC)
    z_hi = lax.rem(role // NC, NZH)
    y = lax.rem(role // (NC * NZH), NY)
    x = role // (NC * NZH * NY)
    return x, y, z_hi, core, z_lo


def device(x, y, z_hi, core, z_lo):
    return (((x * NY + y) * NZH + z_hi) * NC + core, z_lo)


def ring_device(x, y, core, ring):
    return device(x, y, ring // NZL, core, lax.rem(ring, NZL))


def ring_head(ring):
    return 2 * lax.rem(ring, NZL) + ring // NZL


def slot_of(x, y, core):
    return (core * NX + x) * NY + y


def nt_dot(a, b):
    return lax.dot_general(a, b, (((1,), (1,)), ((), ())), preferred_element_type=F32)


def dot(a, b):
    return jnp.dot(a, b, preferred_element_type=F32)


def enter(peers):
    barrier = pltpu.get_barrier_semaphore()
    for peer in peers:
        pl.semaphore_signal(barrier, inc=1, device_id=peer, device_id_type=pl.DeviceIdType.MESH)
    pl.semaphore_wait(barrier, len(peers))


def remote(src, dst, send, recv, peer):
    return pltpu.make_async_remote_copy(
        src_ref=src,
        dst_ref=dst,
        send_sem=send,
        recv_sem=recv,
        device_id=peer,
        device_id_type=pl.DeviceIdType.MESH,
    )


def gather_kernel(
    plen, kv, q, src, ka, kb, qg, srcg, blk_a, blk_b, local, far, send_q, recv_q, send_s, recv_s,
    send_1, recv_1, send_2, recv_2, send_c, recv_c, send_f,
):
    x, y, zh, core, zl = position()
    ring = zh * NZL + zl
    sibling = device(x, y, zh, 1 - core, zl)
    ring_peers = [ring_device(x, y, core, lax.rem(ring + d, RING)) for d in range(1, RING)]
    x_peers = [device(lax.rem(x + d, NX), y, zh, core, zl) for d in range(1, NX)]
    y_peers = [device(x, lax.rem(y + d, NY), zh, core, zl) for d in range(1, NY)]

    row_bias = jnp.where(
        lax.broadcasted_iota(jnp.int32, (16, PRE), 1) < plen[0], 0.0, NEGATIVE
    ).astype(BF16)
    for half in range(2):
        columns = slice(half * HD, (half + 1) * HD)
        blk_a[half] = kv[0, 0, :, columns]
        blk_b[half, 0:KEYS] = kv[0, 1, :, columns]
        blk_b[half, KEYS:] = row_bias

    enter(ring_peers + x_peers + y_peers + [sibling])

    mine = slot_of(x, y, core)
    antipode = ring_peers[RING // 2 - 1]
    far_copies = [
        remote(blk.at[1 - zh], dst.at[mine, zh], send_f.at[i], far.at[i], antipode)
        for i, (blk, dst) in enumerate(((blk_a, ka), (blk_b, kb)))
    ]
    for copy in far_copies:
        copy.start()
    local_copies = [
        pltpu.make_async_copy(blk_a.at[zh], ka.at[mine, zh], local.at[0]),
        pltpu.make_async_copy(blk_b.at[zh], kb.at[mine, zh], local.at[1]),
        pltpu.make_async_copy(q.at[:, ring_head(ring)], qg.at[ring], local.at[2]),
        pltpu.make_async_copy(src, srcg.at[ring], local.at[3]),
    ]
    for copy in local_copies:
        copy.start()
    q_copies = []
    for d in range(1, RING):
        other = lax.rem(ring + d, RING)
        q_copies.append(
            remote(src, srcg.at[ring], send_s.at[d - 1], recv_s.at[d - 1], ring_peers[d - 1])
        )
        q_copies.append(
            remote(
                q.at[:, ring_head(other)],
                qg.at[ring],
                send_q.at[d - 1],
                recv_q.at[d - 1],
                ring_peers[d - 1],
            )
        )
    for copy in q_copies:
        copy.start()

    local_copies[0].wait()
    local_copies[1].wait()
    for copy in far_copies:
        copy.wait_recv()

    paths = ((ka, x_peers, y_peers), (kb, y_peers, x_peers))

    def slot_at(path, first, second):
        if path == 0:
            return slot_of(lax.rem(x + NX - first, NX), lax.rem(y + NY - second, NY), core)
        return slot_of(lax.rem(x + NX - second, NX), lax.rem(y + NY - first, NY), core)

    sent = []

    def push(ref, slot, send, recv, peer):
        copy = remote(ref.at[slot], ref.at[slot], send, recv, peer)
        copy.start()
        sent.append(copy)

    firsts = [[], []]
    seconds = [[], []]
    sides = []
    for path, (ref, first_peers, second_peers) in enumerate(paths):
        for d in range(1, 4):
            push(ref, mine, send_1.at[path, d - 1], recv_1.at[path, d - 1], first_peers[d - 1])
            firsts[path].append(sent[-1])
    for d in range(4):
        for path, (ref, first_peers, second_peers) in enumerate(paths):
            if d > 0:
                firsts[path][d - 1].wait_recv()
            slot = slot_at(path, d, 0)
            for e in range(1, 4):
                push(
                    ref, slot, send_2.at[path, d, e - 1], recv_2.at[path, d, e - 1],
                    second_peers[e - 1],
                )
                seconds[path].append(sent[-1])
            push(ref, slot, send_c.at[path, d, 0], recv_c.at[path, d, 0], sibling)
            sides.append(sent[-1])
    for d in range(4):
        for path, (ref, first_peers, second_peers) in enumerate(paths):
            for e in range(1, 4):
                seconds[path][d * 3 + e - 1].wait_recv()
                push(
                    ref, slot_at(path, d, e), send_c.at[path, d, e], recv_c.at[path, d, e], sibling
                )
                sides.append(sent[-1])
    for copy in sides:
        copy.wait_recv()
    for copy in q_copies:
        copy.wait()
    local_copies[2].wait()
    local_copies[3].wait()
    for copy in far_copies:
        copy.wait_send()
    for copy in sent:
        copy.wait_send()


def prefill_part(plen, prompt_q, kv, prompt_out):
    position_of = lax.broadcasted_iota(jnp.int32, (C, KEYS), 1)
    own_row = lax.broadcasted_iota(jnp.int32, (C, KEYS), 0)
    usable = (position_of < plen[0]) | ((position_of >= PRE) & (position_of - PRE <= own_row))
    for c in range(2):
        keys = kv[0, 0, :, c * HD : (c + 1) * HD]
        values = kv[0, 1, :, c * HD : (c + 1) * HD]
        for g in range(PER_KV):
            columns = slice((c * PER_KV + g) * HD, (c * PER_KV + g + 1) * HD)
            scores = nt_dot(prompt_q[0, :, columns], keys) * SCALE
            scores = jnp.where(usable, scores, NEGATIVE)
            highest = jnp.max(scores, axis=-1, keepdims=True)
            terms = jnp.where(usable, jnp.exp(scores - highest), 0.0)
            total = jnp.sum(terms, axis=-1, keepdims=True)
            weighted = dot(terms.astype(BF16), values)
            prompt_out[0, :, columns] = (weighted / total).astype(BF16)


def local_part(lengths, q, cache, fresh, acc, stats):
    all_rows = KVH * ROWS
    row = lax.broadcasted_iota(jnp.int32, (all_rows, LOCAL_KEYS), 0)
    col = lax.broadcasted_iota(jnp.int32, (all_rows, LOCAL_KEYS), 1)
    in_cache = col < KVH * LOC
    head = row // ROWS
    cache_ok = in_cache & (col // LOC == head)
    fresh_col = col - KVH * LOC
    fresh_ok = (~in_cache) & (fresh_col // STEPS == head) & (fresh_col % STEPS <= row % STEPS)
    rank = jnp.where(cache_ok, col % LOC, jnp.where(fresh_ok, -1, 2 * LOC))
    lane = lax.broadcasted_iota(jnp.int32, (all_rows, 128), 1)

    def body(s, table):
        queries = q[s].reshape(all_rows, HD)
        keys = jnp.concatenate(
            [cache[s, 0, :, h * HD : (h + 1) * HD] for h in range(KVH)] + [fresh[s, 0]], axis=0
        )
        values = jnp.concatenate(
            [cache[s, 1, :, h * HD : (h + 1) * HD] for h in range(KVH)] + [fresh[s, 1]], axis=0
        )
        usable = rank < lengths[s]
        scores = jnp.where(usable, nt_dot(queries, keys) * SCALE, NEGATIVE)
        highest = jnp.max(scores, axis=-1, keepdims=True)
        terms = jnp.where(usable, jnp.exp(scores - highest), 0.0)
        total = jnp.sum(terms, axis=-1, keepdims=True)
        acc[s] = dot(terms.astype(BF16), values)
        table = jnp.where(lane == s, highest, table)
        return jnp.where(lane == s + 64, total, table)

    stats[...] = lax.fori_loop(0, SEQ, body, jnp.zeros((all_rows, 128), F32))


def home_kernel(plen, lengths, prompt_q, kv, q, cache, fresh, prompt_out, acc, stats):
    prefill_part(plen, prompt_q, kv, prompt_out)
    local_part(lengths, q, cache, fresh, acc, stats)


def remote_part(ring, sources, ka, kb, qg, ro, rs):
    lane = lax.broadcasted_iota(jnp.int32, (ROWS, 128), 1)
    group = 8

    def one(s, table):
        prompt = sources[ring * SEQ + s]
        where_at = lax.rem(prompt, NC) * (SLOTS * NZH // NC) + prompt // NC
        slot = where_at // NZH
        half = lax.rem(where_at, NZH)
        keys = ka[slot, half]
        values = kb[slot, half, 0:KEYS]
        bias = kb[slot, half, KEYS:].astype(F32)
        scores = nt_dot(qg[ring, s], keys) * SCALE
        prefix = scores[:, 0:PRE] + bias
        stretch = scores[:, PRE:]
        highest = jnp.maximum(
            jnp.max(prefix, axis=-1, keepdims=True), jnp.max(stretch, axis=-1, keepdims=True)
        )
        terms = jnp.concatenate([jnp.exp(prefix - highest), jnp.exp(stretch - highest)], axis=1)
        total = jnp.sum(terms, axis=-1, keepdims=True)
        ro[ring, s] = (dot(terms.astype(BF16), values) / total).astype(BF16)
        table = jnp.where(lane == s, highest, table)
        return jnp.where(lane == s + 64, total, table)

    def body(block, table):
        for i in range(group):
            table = one(block * group + i, table)
        return table

    rs[ring] = lax.fori_loop(0, SEQ // group, body, jnp.zeros((ROWS, 128), F32))


def remote_kernel(sources, ka, kb, qg, ro, rs):
    def body(ring, carry):
        remote_part(ring, sources, ka, kb, qg, ro, rs)
        return carry

    lax.fori_loop(0, RING, body, 0)


def return_kernel(ro, rs, bo, bs, local, send, recv):
    x, y, zh, core, zl = position()
    ring = zh * NZL + zl
    peers = [ring_device(x, y, core, lax.rem(ring + d, RING)) for d in range(1, RING)]
    enter(peers)
    copies = []
    for d in range(1, RING):
        other = lax.rem(ring + d, RING)
        for i, (source, target) in enumerate(((ro, bo), (rs, bs))):
            copies.append(
                remote(
                    source.at[other], target.at[ring], send.at[i, d - 1], recv.at[i, d - 1],
                    peers[d - 1],
                )
            )
            copies[-1].start()
    own = [
        pltpu.make_async_copy(ro.at[ring], bo.at[ring], local.at[0]),
        pltpu.make_async_copy(rs.at[ring], bs.at[ring], local.at[1]),
    ]
    for copy in own:
        copy.start()
    for copy in own + copies:
        copy.wait()


def merge_part(ring, head, bo, bs, acc, stats, out):
    far = bs[ring]
    rows = slice(head * ROWS, (head + 1) * ROWS)
    near = stats[rows]
    far_sum = pltpu.roll(far, 64, 1)
    near_sum = pltpu.roll(near, 64, 1)
    peak = jnp.maximum(far, near)
    near_scale = jnp.exp(near - peak)
    far_share = far_sum * jnp.exp(far - peak)
    whole = far_share + near_sum * near_scale
    far_weight = far_share / whole
    near_weight = near_scale / whole
    for s in range(SEQ):
        merged = (
            far_weight[:, s : s + 1] * bo[ring, s].astype(F32)
            + near_weight[:, s : s + 1] * acc[s, rows]
        )
        out[s, head] = merged.astype(BF16)


def merge_kernel(bo, bs, acc, stats, out):
    for ring in range(RING):
        merge_part(ring, 2 * (ring % NZL) + ring // NZL, bo, bs, acc, stats, out)


def shards(
    prompt_q, prompt_kv, prefix_length, decode_q, decode_kv, fresh_kv, source_prompt, cache_length
):
    q = decode_q[0].reshape(SEQ, STEPS, HEADS, HD).transpose(0, 2, 1, 3)
    q = q.reshape(SEQ, KVH, ROWS, HD)
    fresh = fresh_kv[0].reshape(SEQ, 2, STEPS, KVH, HD).transpose(0, 1, 3, 2, 4)
    fresh = fresh.reshape(SEQ, 2, KVH * STEPS, HD)
    src = jnp.pad(source_prompt[0, :, 0][None, :], ((0, 0), (0, 128 - SEQ)))
    vmem = pl.BlockSpec(memory_space=VMEM)
    smem = pl.BlockSpec(memory_space=pltpu.SMEM)
    anys = pl.BlockSpec(memory_space=pl.ANY)
    shape = jax.ShapeDtypeStruct
    sem = pltpu.SemaphoreType.DMA
    ka, kb, qg, srcg = pl.pallas_call(
        gather_kernel,
        out_shape=(
            shape((SLOTS, NZH, KEYS, HD), BF16),
            shape((SLOTS, NZH, KEYS + 16, HD), BF16),
            shape((RING, SEQ, ROWS, HD), BF16),
            shape((RING, 1, 128), jnp.int32),
        ),
        in_specs=[smem, vmem, anys, anys],
        out_specs=[anys] * 4,
        scratch_shapes=[
            VMEM((2, KEYS, HD), BF16),
            VMEM((2, KEYS + 16, HD), BF16),
            sem((4,)),
            sem((2,)),
            sem((RING - 1,)),
            sem((RING - 1,)),
            sem((RING - 1,)),
            sem((RING - 1,)),
            sem((2, 3)),
            sem((2, 3)),
            sem((2, 4, 3)),
            sem((2, 4, 3)),
            sem((2, 4, 4)),
            sem((2, 4, 4)),
            sem((2,)),
        ],
        compiler_params=pltpu.CompilerParams(
            collective_id=0, has_side_effects=True, vmem_limit_bytes=8 * MIB
        ),
        name="gather",
    )(prefix_length, prompt_kv, q, src)

    prompt_out, acc, stats = pl.pallas_call(
        home_kernel,
        out_shape=(
            shape((1, C, 2 * PER_KV * HD), BF16),
            shape((SEQ, KVH * ROWS, HD), F32),
            shape((KVH * ROWS, 128), F32),
        ),
        in_specs=[smem, smem, vmem, vmem, vmem, vmem, vmem],
        out_specs=[vmem] * 3,
        compiler_params=pltpu.CompilerParams(vmem_limit_bytes=32 * MIB),
        name="home",
    )(prefix_length, cache_length[0], prompt_q, prompt_kv, q, decode_kv[0], fresh)

    sources = srcg[:, 0, :SEQ].reshape(RING * SEQ)
    ro, rs = pl.pallas_call(
        remote_kernel,
        out_shape=(
            shape((RING, SEQ, ROWS, HD), BF16),
            shape((RING, ROWS, 128), F32),
        ),
        in_specs=[smem, vmem, vmem, vmem],
        out_specs=[vmem] * 2,
        compiler_params=pltpu.CompilerParams(vmem_limit_bytes=32 * MIB),
        name="attend",
    )(sources, ka, kb, qg)

    bo, bs = pl.pallas_call(
        return_kernel,
        out_shape=(
            shape((RING, SEQ, ROWS, HD), BF16),
            shape((RING, ROWS, 128), F32),
        ),
        in_specs=[anys] * 2,
        out_specs=[anys] * 2,
        scratch_shapes=[sem((2,)), sem((2, RING - 1)), sem((2, RING - 1))],
        compiler_params=pltpu.CompilerParams(
            collective_id=1, has_side_effects=True, vmem_limit_bytes=8 * MIB
        ),
        name="giveback",
    )(ro, rs)

    out = pl.pallas_call(
        merge_kernel,
        out_shape=shape((SEQ, KVH, ROWS, HD), BF16),
        in_specs=[vmem] * 4,
        out_specs=vmem,
        compiler_params=pltpu.CompilerParams(vmem_limit_bytes=32 * MIB),
        name="merge",
    )(bo, bs, acc, stats)
    out = out.reshape(SEQ, HEADS, STEPS, HD).transpose(0, 2, 1, 3)
    return prompt_out, out.reshape(1, SEQ, STEPS, HEADS * HD)


def solution(mesh):
    return jax.shard_map(
        shards,
        mesh=mesh,
        in_specs=(
            P("role", None, "tp"),
            P("role", None, None, "tp"),
            P("role"),
            P("role", "tp", None, None),
            P("role", "tp", None, None, None),
            P("role", "tp", None, None, None),
            P("role", "tp", None),
            P("role", "tp"),
        ),
        out_specs=(P("role", None, "tp"), P("role", "tp", None, None)),
        check_vma=False,
    )
```

time: 832 us -> 175 us (0.21)
  waiting for transfers between devices: 363 us -> 0 us
  Pallas kernels: 0 us -> 165 us
  local copies, waits for them, and re-layouts: 164 us -> 8.64 us
  starting transfers between devices: 131 us -> 0 us
  blocking collectives: 116 us -> 0 us
  matrix products: 31.1 us -> 0 us
  other arithmetic: 17.4 us -> 0 us
    all_to_all x7 -> x0, waiting for transfers between devices: 363 us -> none  [the longest x1 149 us: shards(): lax.all_to_all(lax.all_to_all(remote_out, 'role', split_axis=0, concat_ax...]
    pallas_call x0 -> x5, Pallas kernels: none -> 165 us  [the longest x1 69.6 us: shards(): pl.pallas_call(remote_kernel, out_shape=(shape((RING, SEQ, ROWS, HD), BF1...]
    all_to_all x7 -> x0, starting transfers between devices: 131 us -> none  [the longest x1 102 us: shards(): lax.all_to_all(lax.all_to_all(remote_max, 'role', split_axis=0, concat_ax...]
    all_to_all x1 -> x0, blocking collectives: 116 us -> none  [shards(): lax.all_to_all(outgoing, 'role', split_axis=0, concat_axis=0, tiled=True)]
    all_to_all x7 -> x0, local copies, waits for them, and re-layouts: 53.5 us -> none  [the longest x1 15.4 us: shards(): lax.all_to_all(lax.all_to_all(remote_out, 'role', split_axis=0, concat_ax...]
    reshape x12 -> x0, local copies, waits for them, and re-layouts: 48.2 us -> none  [the longest x2 14.3 us: shards(): outgoing.reshape(role_count, capacity, step_count, tp_count, feature_widt...]
    dot_general x22 -> x0, matrix products: 29.8 us -> none  [the longest x8 6.32 us: remote_every(): jnp.einsum('rcgt,tcd->rcgd', weights, prompt_values, preferred_element_ty...]
    dynamic_update_slice x16 -> x0, local copies, waits for them, and re-layouts: 12.9 us -> none  [shards(): remote_out, remote_max, remote_sum = lax.map(answer, asked_rows)]
  transfers between devices with their start and end apart: 7 -> 0, of which waited for: 5 -> 0; matrix products, arithmetic and copies ran while one was open for 8% -> 0% of each run, Pallas kernels for 0% -> 0%
where the time goes in v1:
time: 175 us
  Pallas kernels  165 us (94%)
  local copies, waits for them, and re-layouts  8.64 us (5%)
    pallas_call x1, Pallas kernels, shards(): pl.pallas_call(remote_kernel, out_shape=(shape((RING, SEQ, ROWS, HD), BF1...  69.6 us
    pallas_call x1, Pallas kernels, shards(): pl.pallas_call(gather_kernel, out_shape=(shape((SLOTS, NZH, KEYS, HD), BF...  42.7 us
    pallas_call x1, Pallas kernels, shards(): pl.pallas_call(return_kernel, out_shape=(shape((RING, SEQ, ROWS, HD), BF1...  30.9 us
    pallas_call x1, Pallas kernels, shards(): pl.pallas_call(home_kernel, out_shape=(shape((1, C, 2 * PER_KV * HD), BF1...  17.9 us
    unnamed x24, local copies, waits for them, and re-layouts  7.89 us
    pallas_call x1, Pallas kernels, shards(): pl.pallas_call(merge_kernel, out_shape=shape((SEQ, KVH, ROWS, HD), BF16),...  3.79 us

profile of v1, /device:TPU:1, one launch (start us, length us, event | category | flops | bytes accessed | tf_op | source)
XLA Modules:
  0.0 175.0 jit_solution(3307091653660883608)
XLA Ops:
  1.3 0.7 pad.4.src
  1.9 0.0 copy-start
  1.9 1.2 copy-done
  3.2 0.0 copy-start.7
  3.2 0.9 copy-done.7
  4.1 42.7 %gather.1 = (bf16[32,2,192,128]{3,2,1,0:T(8,128)(2,1)S(1)}, bf16[32,2,208,128]{3,2,1,0:T(8,128)(2,1)S(1)}, bf16[8,32,16,128]{3,2,1,0:T(8,128)(2,1)S(1)}, s32[8,1,128]{2,1,0:T(1,128)S(1)}) custom-call(s32[1]{0:T(128)S(6)} %copy.13.plen, bf16[1,2,192,256]{3,2,1,0:T(8,128)(2,1)S(1)} %copy-done.7, bf16[32,8,16,128]{3,2,1,0:T(8,128)(2,1)S(1)} %bitcast.18, ...), custom_call_target="tpu_custom_call" | custom-call | tf_op jit(solution)/shard_map/gather/pallas_call | solution.py:361
  46.8 0.0 copy-start.2
  46.8 1.6 copy-done.2
  48.5 1.0 copy-done.5
  49.4 0.1 reshape_squeeze.11.sources
  49.5 1.9 %copy-done.3 = bf16[32,2,192,128]{3,2,1,0:T(8,128)(2,1)S(1)} copy-done((bf16[32,2,192,128]{3,2,1,0:T(8,128)(2,1)S(1)}, bf16[32,2,192,128]{3,2,1,0:T(8,128)(2,1)}, u32[]{:S(2)}) %copy-start.3) | copy-done | bytes 3145752
  51.4 1.2 copy-done.6
  52.6 0.0 copy-start.10
  52.7 0.0 copy-start.11
  52.7 69.6 %attend.1 = (bf16[8,32,16,128]{3,2,1,0:T(8,128)(2,1)S(1)}, f32[8,16,128]{2,1,0:T(8,128)S(1)}) custom-call(s32[256]{0:T(256)S(1)} %reshape_squeeze.11.sources, bf16[32,2,192,128]{3,2,1,0:T(8,128)(2,1)S(1)} %copy-done.3, bf16[32,2,208,128]{3,2,1,0:T(8,128)(2,1)S(1)} %get-tuple-element.16.kb, bf16[8,32,16,128]{3,2,1,0:T(8,128)(2,1)S(1)} %copy-done.6), custom_call_target="tpu_custom_call" | custom-call | tf_op jit(solution)/shard_map/attend/pallas_call | solution.py:408
  122.2 30.9 %giveback.1 = (bf16[8,32,16,128]{3,2,1,0:T(8,128)(2,1)S(1)}, f32[8,16,128]{2,1,0:T(8,128)S(1)}) custom-call(bf16[8,32,16,128]{3,2,1,0:T(8,128)(2,1)S(1)} %get-tuple-element.18.ro, f32[8,16,128]{2,1,0:T(8,128)S(1)} %get-tuple-element.19.rs), custom_call_target="tpu_custom_call" | custom-call | tf_op jit(solution)/shard_map/giveback/pallas_call | solution.py:420
  153.2 0.0 copy-done.1
  153.2 0.0 copy-done.4
  153.2 0.0 copy-done.8
  153.2 0.0 copy-done.9
  153.2 0.0 copy-done.10
  153.2 0.0 copy-done.11
  153.2 17.9 %home.1 = (bf16[1,64,2048]{2,1,0:T(8,128)(2,1)}, f32[32,128,128]{2,1,0:T(8,128)S(1)}, f32[128,128]{1,0:T(8,128)S(1)}) custom-call(s32[1]{0:T(128)S(6)} %copy.13.plen, s32[32]{0:T(128)S(1)} %bitcast.22, bf16[1,64,2048]{2,1,0:T(8,128)(2,1)S(1)} %copy-done.9, bf16[1,2,192,256]{3,2,1,0:T(8,128)(2,1)S(1)} %copy-done.8, bf16[32,8,16,128]{3,2,1,0:T(8,128)(2,1)S(1)} %bitcast.19, ...), custom_call_target="tpu_custom_call" | custom-call | tf_op jit(solution)/shard_map/home/pallas_call | solution.py:394
  171.2 3.8 %merge.1 = bf16[32,8,16,128]{3,2,1,0:T(8,128)(2,1)} custom-call(bf16[8,32,16,128]{3,2,1,0:T(8,128)(2,1)S(1)} %get-tuple-element.20.bo, f32[8,16,128]{2,1,0:T(8,128)S(1)} %get-tuple-element.21.bs, f32[32,128,128]{2,1,0:T(8,128)S(1)} %get-tuple-element.22.acc, f32[128,128]{1,0:T(8,128)S(1)} %get-tuple-element.23.stats), custom_call_target="tpu_custom_call" | custom-call | tf_op jit(solution)/shard_map/merge/pallas_call | solution.py:435
  (8 shorter events, 0.0 us)
Async XLA Ops:
  1.9 1.2 copy-start
  3.2 0.9 copy-start.7
  46.8 1.6 copy-start.2
  48.5 1.0 copy-start.5
  49.5 1.9 %copy-start.3 = (bf16[32,2,192,128]{3,2,1,0:T(8,128)(2,1)S(1)}, bf16[32,2,192,128]{3,2,1,0:T(8,128)(2,1)}, u32[]{:S(2)}) copy-start(bf16[32,2,192,128]{3,2,1,0:T(8,128)(2,1)} %copy-done.2) | copy-start | bytes 9437188
  51.4 1.2 copy-start.6
  52.6 100.6 %copy-start.1 = (bf16[1,32,2,8192]{3,2,1,0:T(2,128)(2,1)S(1)}, bf16[1,32,2,8192]{3,2,1,0:T(2,128)(2,1)}, u32[]{:S(2)}) copy-start(bf16[1,32,2,8192]{3,2,1,0:T(2,128)(2,1)} %param.11) | copy-start | bytes 3145732
  52.6 100.6 %copy-start.4 = (bf16[1,32,2,16,1024]{4,3,2,1,0:T(8,128)(2,1)S(1)}, bf16[1,32,2,16,1024]{4,3,2,1,0:T(8,128)(2,1)}, u32[]{:S(2)}) copy-start(bf16[1,32,2,16,1024]{4,3,2,1,0:T(8,128)(2,1)} %param.12) | copy-start | bytes 6291460
  52.6 100.6 %copy-start.8 = (bf16[1,2,192,256]{3,2,1,0:T(8,128)(2,1)S(1)}, bf16[1,2,192,256]{3,2,1,0:T(8,128)(2,1)}, u32[]{:S(2)}) copy-start(bf16[1,2,192,256]{3,2,1,0:T(8,128)(2,1)} %kv.3) | copy-start | bytes 589828
  52.6 100.6 %copy-start.9 = (bf16[1,64,2048]{2,1,0:T(8,128)(2,1)S(1)}, bf16[1,64,2048]{2,1,0:T(8,128)(2,1)}, u32[]{:S(2)}) copy-start(bf16[1,64,2048]{2,1,0:T(8,128)(2,1)} %prompt_q.1) | copy-start | bytes 786436
  52.6 100.6 %copy-start.10 = (bf16[1,32,2,2,1024]{4,3,2,1,0:T(2,128)(2,1)S(1)}, bf16[1,32,2,2,1024]{4,3,2,1,0:T(2,128)(2,1)}, u32[]{:S(2)}) copy-start(bf16[1,32,2,2,1024]{4,3,2,1,0:T(2,128)(2,1)} %param.13) | copy-start | bytes 786436
  52.7 100.6 %copy-start.11 = (s32[1,32]{1,0:T(1,128)S(1)}, s32[1,32]{1,0:T(1,128)}, u32[]{:S(2)}) copy-start(s32[1,32]{1,0:T(1,128)} %param.15) | copy-start | bytes 388

commit v2 on v1

v2 whole, which is shorter than its diff:
```python
import math

import jax
import jax.numpy as jnp
from jax import lax
from jax.experimental import pallas as pl
from jax.experimental.pallas import tpu as pltpu
from jax.sharding import PartitionSpec as P

HEADS = 64
KVH = 8
PER_KV = HEADS // KVH
HD = 128
C = 64
PRE = 128
KEYS = PRE + C
LOC = 16
SEQ = 32
STEPS = 2
ROWS = PER_KV * STEPS
NX, NY, NZH, NC, NZL = 4, 4, 2, 2, 4
RING = NZH * NZL
SLOTS = NC * NX * NY
SCALE = 1.0 / math.sqrt(HD)
NEGATIVE = -1e30
LOCAL_KEYS = KVH * (LOC + STEPS)

F32 = jnp.float32
BF16 = jnp.bfloat16
VMEM = pltpu.VMEM
MIB = 1024 * 1024


def position():
    role = lax.axis_index("role")
    z_lo = lax.axis_index("tp")
    core = lax.rem(role, NC)
    z_hi = lax.rem(role // NC, NZH)
    y = lax.rem(role // (NC * NZH), NY)
    x = role // (NC * NZH * NY)
    return x, y, z_hi, core, z_lo


def device(x, y, z_hi, core, z_lo):
    return (((x * NY + y) * NZH + z_hi) * NC + core, z_lo)


def ring_device(x, y, core, ring):
    return device(x, y, ring // NZL, core, lax.rem(ring, NZL))


def ring_head(ring):
    return 2 * lax.rem(ring, NZL) + ring // NZL


def slot_of(x, y, core):
    return (core * NX + x) * NY + y


def nt_dot(a, b):
    return lax.dot_general(a, b, (((1,), (1,)), ((), ())), preferred_element_type=F32)


def dot(a, b):
    return jnp.dot(a, b, preferred_element_type=F32)


def enter(peers):
    barrier = pltpu.get_barrier_semaphore()
    for peer in peers:
        pl.semaphore_signal(barrier, inc=1, device_id=peer, device_id_type=pl.DeviceIdType.MESH)
    pl.semaphore_wait(barrier, len(peers))


def remote(src, dst, send, recv, peer):
    return pltpu.make_async_remote_copy(
        src_ref=src,
        dst_ref=dst,
        send_sem=send,
        recv_sem=recv,
        device_id=peer,
        device_id_type=pl.DeviceIdType.MESH,
    )


def prefill_part(c, plen, prompt_q, blk_a, blk_b, prompt_out):
    position_of = lax.broadcasted_iota(jnp.int32, (C, KEYS), 1)
    own_row = lax.broadcasted_iota(jnp.int32, (C, KEYS), 0)
    usable = (position_of < plen[0]) | ((position_of >= PRE) & (position_of - PRE <= own_row))
    keys = blk_a[c]
    values = blk_b[c, 0:KEYS]
    for g in range(PER_KV):
        columns = slice((c * PER_KV + g) * HD, (c * PER_KV + g + 1) * HD)
        scores = nt_dot(prompt_q[0, :, columns], keys) * SCALE
        scores = jnp.where(usable, scores, NEGATIVE)
        highest = jnp.max(scores, axis=-1, keepdims=True)
        terms = jnp.where(usable, jnp.exp(scores - highest), 0.0)
        total = jnp.sum(terms, axis=-1, keepdims=True)
        weighted = dot(terms.astype(BF16), values)
        prompt_out[0, :, columns] = (weighted / total).astype(BF16)


def local_part(first, last, lengths, q, cache, fresh, acc, stats):
    all_rows = KVH * ROWS
    row = lax.broadcasted_iota(jnp.int32, (all_rows, LOCAL_KEYS), 0)
    col = lax.broadcasted_iota(jnp.int32, (all_rows, LOCAL_KEYS), 1)
    in_cache = col < KVH * LOC
    head = row // ROWS
    cache_ok = in_cache & (col // LOC == head)
    fresh_col = col - KVH * LOC
    fresh_ok = (~in_cache) & (fresh_col // STEPS == head) & (fresh_col % STEPS <= row % STEPS)
    rank = jnp.where(cache_ok, col % LOC, jnp.where(fresh_ok, -1, 2 * LOC))
    lane = lax.broadcasted_iota(jnp.int32, (all_rows, 128), 1)
    group = 2

    def rows_of(s, which):
        return jnp.concatenate(
            [cache[s, which, :, h * HD : (h + 1) * HD] for h in range(KVH)] + [fresh[s, which]],
            axis=0,
        )

    def body(block, table):
        seqs = [block * group + i for i in range(group)]
        usable = [rank < lengths[s] for s in seqs]
        scores = [nt_dot(q[s].reshape(all_rows, HD), rows_of(s, 0)) for s in seqs]
        scores = [jnp.where(u, x * SCALE, NEGATIVE) for u, x in zip(usable, scores)]
        highest = [jnp.max(x, axis=-1, keepdims=True) for x in scores]
        terms = [
            jnp.where(u, jnp.exp(x - h), 0.0) for u, x, h in zip(usable, scores, highest)
        ]
        total = [jnp.sum(x, axis=-1, keepdims=True) for x in terms]
        weighted = [dot(x.astype(BF16), rows_of(s, 1)) for x, s in zip(terms, seqs)]
        for i, s in enumerate(seqs):
            acc[s] = weighted[i]
            table = jnp.where(lane == s, highest[i], table)
            table = jnp.where(lane == s + 64, total[i], table)
        return table

    start = jnp.zeros((all_rows, 128), F32) if first == 0 else stats[...]
    stats[...] = lax.fori_loop(first // group, last // group, body, start)


def remote_part(ring, sources, ka, kb, qg, ro, rs):
    lane = lax.broadcasted_iota(jnp.int32, (ROWS, 128), 1)
    group = 16

    def body(block, table):
        seqs = [block * group + i for i in range(group)]
        places = []
        for s in seqs:
            prompt = sources[ring, 0, s]
            slot = lax.rem(prompt, NC) * (SLOTS // NC) + prompt // (NC * NZH)
            places.append((slot, lax.rem(prompt // NC, NZH)))
        scores = jnp.concatenate(
            [nt_dot(qg[ring, s], ka[slot, half]) for s, (slot, half) in zip(seqs, places)], axis=0
        )
        scores = scores * SCALE
        bias = jnp.concatenate([kb[slot, half, KEYS:] for slot, half in places], axis=0)
        prefix = scores[:, 0:PRE] + bias.astype(F32)
        stretch = scores[:, PRE:]
        highest = jnp.maximum(
            jnp.max(prefix, axis=-1, keepdims=True), jnp.max(stretch, axis=-1, keepdims=True)
        )
        terms = jnp.concatenate([jnp.exp(prefix - highest), jnp.exp(stretch - highest)], axis=1)
        total = jnp.sum(terms, axis=-1, keepdims=True)
        weights = terms.astype(BF16)
        for i, (s, (slot, half)) in enumerate(zip(seqs, places)):
            rows = slice(i * ROWS, (i + 1) * ROWS)
            weighted = dot(weights[rows], kb[slot, half, 0:KEYS])
            ro[ring, s] = (weighted / total[rows]).astype(BF16)
            table = jnp.where(lane == s, highest[rows], table)
            table = jnp.where(lane == s + 64, total[rows], table)
        return table

    rs[ring] = lax.fori_loop(0, SEQ // group, body, jnp.zeros((ROWS, 128), F32))


def merge_part(ring, bo, bs, acc, stats, out):
    head = ring_head(ring)
    far = bs[ring]
    rows = pl.ds(pl.multiple_of(head * ROWS, ROWS), ROWS)
    near = stats[rows]
    far_sum = pltpu.roll(far, 64, 1)
    near_sum = pltpu.roll(near, 64, 1)
    peak = jnp.maximum(far, near)
    near_scale = jnp.exp(near - peak)
    far_share = far_sum * jnp.exp(far - peak)
    whole = far_share + near_sum * near_scale
    far_weight = far_share / whole
    near_weight = near_scale / whole
    for s in range(SEQ):
        merged = (
            far_weight[:, s : s + 1] * bo[ring, s].astype(F32)
            + near_weight[:, s : s + 1] * acc[s, rows]
        )
        out[s, head] = merged.astype(BF16)


def kernel(
    plen, lengths, prompt_q_hbm, kv, q, cache_hbm, fresh_hbm, src, prompt_out, out,
    blk_a, blk_b, ka, kb, qg, srcg, sources, ro, rs, bo, bs, acc, stats,
    prompt_q, q_own, cache, fresh, load, local,
    send_q, recv_q, send_s, recv_s, send_f, recv_f, send_1, recv_1, send_2, recv_2, send_c, recv_c,
    send_o, recv_o, send_t, recv_t,
):
    x, y, zh, core, zl = position()
    ring = zh * NZL + zl
    sibling = device(x, y, zh, 1 - core, zl)
    ring_peers = [ring_device(x, y, core, lax.rem(ring + d, RING)) for d in range(1, RING)]
    x_peers = [device(lax.rem(x + d, NX), y, zh, core, zl) for d in range(1, NX)]
    y_peers = [device(x, lax.rem(y + d, NY), zh, core, zl) for d in range(1, NY)]

    blocks = []
    for half in range(2):
        columns = slice(half * HD, (half + 1) * HD)
        blocks.append(
            pltpu.make_async_copy(kv.at[0, 0, :, columns], blk_a.at[half], load.at[half])
        )
        blocks.append(
            pltpu.make_async_copy(
                kv.at[0, 1, :, columns], blk_b.at[half, 0:KEYS], load.at[2 + half]
            )
        )
    loads = [
        pltpu.make_async_copy(prompt_q_hbm, prompt_q, load.at[4]),
        pltpu.make_async_copy(q, q_own, load.at[5]),
        pltpu.make_async_copy(cache_hbm, cache, load.at[6]),
        pltpu.make_async_copy(fresh_hbm, fresh, load.at[7]),
    ]
    for copy in blocks:
        copy.start()
    row_bias = jnp.where(
        lax.broadcasted_iota(jnp.int32, (16, PRE), 1) < plen[0], 0.0, NEGATIVE
    ).astype(BF16)
    for half in range(2):
        blk_b[half, KEYS:] = row_bias
    enter(ring_peers + x_peers + y_peers + [sibling])
    for copy in blocks:
        copy.wait()

    mine = slot_of(x, y, core)
    antipode = ring_peers[RING // 2 - 1]
    far_copies = [
        remote(blk.at[1 - zh], dst.at[mine, zh], send_f.at[i], recv_f.at[i], antipode)
        for i, (blk, dst) in enumerate(((blk_a, ka), (blk_b, kb)))
    ]
    for copy in far_copies:
        copy.start()
    local_copies = [
        pltpu.make_async_copy(blk_a.at[zh], ka.at[mine, zh], local.at[0]),
        pltpu.make_async_copy(blk_b.at[zh], kb.at[mine, zh], local.at[1]),
        pltpu.make_async_copy(q.at[:, ring_head(ring)], qg.at[ring], local.at[2]),
        pltpu.make_async_copy(src, srcg.at[ring], local.at[3]),
    ]
    for copy in local_copies:
        copy.start()
    q_copies = []
    for d in (4, 3, 5, 2, 6, 1, 7):
        other = lax.rem(ring + d, RING)
        q_copies.append(
            remote(src, srcg.at[ring], send_s.at[d - 1], recv_s.at[d - 1], ring_peers[d - 1])
        )
        q_copies.append(
            remote(
                q.at[:, ring_head(other)],
                qg.at[ring],
                send_q.at[d - 1],
                recv_q.at[d - 1],
                ring_peers[d - 1],
            )
        )
    for copy in q_copies:
        copy.start()
    for copy in loads:
        copy.start()

    loads[0].wait()
    prefill_part(0, plen, prompt_q, blk_a, blk_b, prompt_out)
    local_copies[0].wait()
    local_copies[1].wait()
    for copy in far_copies:
        copy.wait_recv()

    paths = ((ka, x_peers, y_peers), (kb, y_peers, x_peers))

    def slot_at(path, first, second):
        if path == 0:
            return slot_of(lax.rem(x + NX - first, NX), lax.rem(y + NY - second, NY), core)
        return slot_of(lax.rem(x + NX - second, NX), lax.rem(y + NY - first, NY), core)

    sent = []

    def push(ref, slot, send, recv, peer):
        copy = remote(ref.at[slot], ref.at[slot], send, recv, peer)
        copy.start()
        sent.append(copy)

    firsts = [[], []]
    seconds = [[], []]
    sides = []
    for path, (ref, first_peers, second_peers) in enumerate(paths):
        for d in range(1, 4):
            push(ref, mine, send_1.at[path, d - 1], recv_1.at[path, d - 1], first_peers[d - 1])
            firsts[path].append(sent[-1])
    for d in range(4):
        for path, (ref, first_peers, second_peers) in enumerate(paths):
            if d > 0:
                firsts[path][d - 1].wait_recv()
            slot = slot_at(path, d, 0)
            for e in range(1, 4):
                push(
                    ref, slot, send_2.at[path, d, e - 1], recv_2.at[path, d, e - 1],
                    second_peers[e - 1],
                )
                seconds[path].append(sent[-1])
            push(ref, slot, send_c.at[path, d, 0], recv_c.at[path, d, 0], sibling)
            sides.append(sent[-1])
        if d == 0:
            prefill_part(1, plen, prompt_q, blk_a, blk_b, prompt_out)
    for copy in loads[1:]:
        copy.wait()
    for d in range(4):
        local_part(d * 8, d * 8 + 8, lengths, q_own, cache, fresh, acc, stats)
        for path, (ref, first_peers, second_peers) in enumerate(paths):
            for e in range(1, 4):
                seconds[path][d * 3 + e - 1].wait_recv()
                push(
                    ref, slot_at(path, d, e), send_c.at[path, d, e], recv_c.at[path, d, e], sibling
                )
                sides.append(sent[-1])
    for copy in q_copies:
        copy.wait_recv()
    local_copies[2].wait()
    local_copies[3].wait()
    place = pltpu.make_async_copy(srcg, sources, local.at[4])
    place.start()
    place.wait()
    for copy in sides:
        copy.wait_recv()

    def answers(d):
        other = lax.rem(ring + d, RING)
        return [
            remote(
                ro.at[other], bo.at[ring], send_o.at[d], recv_o.at[d],
                ring_device(x, y, core, other),
            ),
            remote(
                rs.at[other], bs.at[ring], send_t.at[d], recv_t.at[d],
                ring_device(x, y, core, other),
            ),
        ]

    def distance(k):
        return RING // 2 + (1 - 2 * lax.rem(k, 2)) * ((k + 1) // 2)

    def answer(k, carry):
        d = distance(k)
        remote_part(lax.rem(ring + d, RING), sources, ka, kb, qg, ro, rs)

        @pl.when(k < RING - 1)
        def _():
            for copy in answers(d):
                copy.start()

        return carry

    lax.fori_loop(0, RING, answer, 0)
    bo[ring] = ro[ring]
    bs[ring] = rs[ring]

    def merge(k, carry):
        d = distance(k)

        @pl.when(k < RING - 1)
        def _():
            for copy in answers(d):
                copy.wait()

        merge_part(lax.rem(ring + RING - d, RING), bo, bs, acc, stats, out)
        return carry

    lax.fori_loop(0, RING, merge, 0)
    for copy in q_copies:
        copy.wait_send()
    for copy in far_copies:
        copy.wait_send()
    for copy in sent:
        copy.wait_send()


def shards(
    prompt_q, prompt_kv, prefix_length, decode_q, decode_kv, fresh_kv, source_prompt, cache_length
):
    q = decode_q[0].reshape(SEQ, STEPS, HEADS, HD).transpose(0, 2, 1, 3)
    q = q.reshape(SEQ, KVH, ROWS, HD)
    fresh = fresh_kv[0].reshape(SEQ, 2, STEPS, KVH, HD).transpose(0, 1, 3, 2, 4)
    fresh = fresh.reshape(SEQ, 2, KVH * STEPS, HD)
    src = jnp.pad(source_prompt[0, :, 0][None, :], ((0, 0), (0, 128 - SEQ)))
    vmem = pl.BlockSpec(memory_space=VMEM)
    smem = pl.BlockSpec(memory_space=pltpu.SMEM)
    anys = pl.BlockSpec(memory_space=pl.ANY)
    shape = jax.ShapeDtypeStruct
    sem = pltpu.SemaphoreType.DMA
    prompt_out, out = pl.pallas_call(
        kernel,
        out_shape=(
            shape((1, C, 2 * PER_KV * HD), BF16),
            shape((SEQ, KVH, ROWS, HD), BF16),
        ),
        in_specs=[smem, smem, anys, anys, anys, anys, anys, anys],
        out_specs=[vmem] * 2,
        scratch_shapes=[
            VMEM((2, KEYS, HD), BF16),
            VMEM((2, KEYS + 16, HD), BF16),
            VMEM((SLOTS, NZH, KEYS, HD), BF16),
            VMEM((SLOTS, NZH, KEYS + 16, HD), BF16),
            VMEM((RING, SEQ, ROWS, HD), BF16),
            VMEM((RING, 1, 128), jnp.int32),
            pltpu.SMEM((RING, 1, 128), jnp.int32),
            VMEM((RING, SEQ, ROWS, HD), BF16),
            VMEM((RING, ROWS, 128), F32),
            VMEM((RING, SEQ, ROWS, HD), BF16),
            VMEM((RING, ROWS, 128), F32),
            VMEM((SEQ, KVH * ROWS, HD), F32),
            VMEM((KVH * ROWS, 128), F32),
            VMEM((1, C, 2 * PER_KV * HD), BF16),
            VMEM((SEQ, KVH, ROWS, HD), BF16),
            VMEM((SEQ, 2, LOC, KVH * HD), BF16),
            VMEM((SEQ, 2, KVH * STEPS, HD), BF16),
            sem((8,)),
            sem((5,)),
        ]
        + [sem((RING - 1,))] * 4
        + [sem((2,))] * 2
        + [sem((2, 3))] * 2
        + [sem((2, 4, 3))] * 2
        + [sem((2, 4, 4))] * 2
        + [sem((RING,))] * 4,
        compiler_params=pltpu.CompilerParams(
            collective_id=0, has_side_effects=True, vmem_limit_bytes=58 * MIB
        ),
        name="attention",
    )(prefix_length, cache_length[0], prompt_q, prompt_kv, q, decode_kv[0], fresh, src)
    out = out.reshape(SEQ, HEADS, STEPS, HD).transpose(0, 2, 1, 3)
    return prompt_out, out.reshape(1, SEQ, STEPS, HEADS * HD)


def solution(mesh):
    return jax.shard_map(
        shards,
        mesh=mesh,
        in_specs=(
            P("role", None, "tp"),
            P("role", None, None, "tp"),
            P("role"),
            P("role", "tp", None, None),
            P("role", "tp", None, None, None),
            P("role", "tp", None, None, None),
            P("role", "tp", None),
            P("role", "tp"),
        ),
        out_specs=(P("role", None, "tp"), P("role", "tp", None, None)),
        check_vma=False,
    )
```

time: 175 us -> 83.6 us (0.48)
  Pallas kernels: 165 us -> 75.8 us
  local copies, waits for them, and re-layouts: 8.64 us -> 6.28 us
    pallas_call x5 -> x1, Pallas kernels: 165 us -> 75.8 us  [shards(): pl.pallas_call(kernel, out_shape=(shape((1, C, 2 * PER_KV * HD), BF16), s...]
    unnamed x24 -> x2, local copies, waits for them, and re-layouts: 7.89 us -> 5.11 us
where the time goes in v2:
time: 83.6 us; the launch traced here: 83.4 us
  Pallas kernels  75.8 us (91%)
  local copies, waits for them, and re-layouts  6.28 us (8%)
  between operations  1.29 us (2%)
    pallas_call x1, Pallas kernels, shards(): pl.pallas_call(kernel, out_shape=(shape((1, C, 2 * PER_KV * HD), BF16), s...  75.8 us
    unnamed x2, local copies, waits for them, and re-layouts  5.11 us

profile of v2, /device:TPU:1, one launch (start us, length us, event | category | flops | bytes accessed | tf_op | source)
XLA Modules:
  0.0 83.4 jit_solution(6990927141255293075)
XLA Ops:
  1.3 1.2 %pad.4.src = s32[1,128]{1,0:T(1,128)} pad(s32[1,32]{1,0:T(1,128)} %bitcast.23, s32[]{:T(128)} %constant.0.clone.1), padding=0_0x0_96 | pad | bytes 644 | tf_op jit(solution)/shard_map/jit(_pad)/pad | solution.py:399
  2.4 75.8 %attention.1 = (bf16[1,64,2048]{2,1,0:T(8,128)(2,1)}, bf16[32,8,16,128]{3,2,1,0:T(8,128)(2,1)}) custom-call(s32[1]{0:T(128)S(6)} %copy.15.plen, s32[32]{0:T(128)} %bitcast.22, bf16[1,64,2048]{2,1,0:T(8,128)(2,1)} %prompt_q_hbm.1, bf16[1,2,192,256]{3,2,1,0:T(8,128)(2,1)} %kv.1, bf16[32,8,16,128]{3,2,1,0:T(8,128)(2,1)} %bitcast.19, ...), custom_call_target="tpu_custom_call" | custom-call | tf_op jit(solution)/shard_map/attention/pallas_call | solution.py:405
  78.3 1.7 %copy.16 = bf16[1,64,2048]{2,1,0:T(8,128)(2,1)} copy(bf16[1,64,2048]{2,1,0:T(8,128)(2,1)} %get-tuple-element.8) | data formatting | bytes 524288
  80.0 3.4 %copy.17 = bf16[1,32,2,8192]{3,2,1,0:T(2,128)(2,1)} copy(bf16[1,32,2,8192]{3,2,1,0:T(2,128)(2,1)} %bitcast.20) | data formatting | bytes 2097152

commit v3 on v2

--- a/solution.py
+++ b/solution.py
@@ -23,6 +23,7 @@
 SLOTS = NC * NX * NY
 SCALE = 1.0 / math.sqrt(HD)
 NEGATIVE = -1e30
+PARTS = 4
 LOCAL_KEYS = KVH * (LOC + STEPS)
 
 F32 = jnp.float32
@@ -172,12 +173,14 @@
             table = jnp.where(lane == s + 64, total[rows], table)
         return table
 
-    rs[ring] = lax.fori_loop(0, SEQ // group, body, jnp.zeros((ROWS, 128), F32))
+    table = lax.fori_loop(0, SEQ // group, body, jnp.zeros((ROWS, 128), F32))
+    rs[ring] = table[0:8] + pltpu.roll(table[8:16], SEQ, 1)
 
 
 def merge_part(ring, bo, bs, acc, stats, out):
     head = ring_head(ring)
-    far = bs[ring]
+    packed = bs[ring]
+    far = jnp.concatenate([packed, pltpu.roll(packed, 128 - SEQ, 1)], axis=0)
     rows = pl.ds(pl.multiple_of(head * ROWS, ROWS), ROWS)
     near = stats[rows]
     far_sum = pltpu.roll(far, 64, 1)
@@ -389,6 +392,22 @@
         copy.wait_send()
 
 
+def copy_kernel(a, b, out_a, out_b, stage_a, stage_b, sem_in, sem_out):
+    loads = [pltpu.make_async_copy(a, stage_a, sem_in.at[PARTS])]
+    stores = [pltpu.make_async_copy(stage_a, out_a, sem_out.at[PARTS])]
+    for i in range(PARTS):
+        rows = pl.ds(i * (SEQ // PARTS), SEQ // PARTS)
+        loads.append(pltpu.make_async_copy(b.at[rows], stage_b.at[rows], sem_in.at[i]))
+        stores.append(pltpu.make_async_copy(stage_b.at[rows], out_b.at[rows], sem_out.at[i]))
+    for copy in loads:
+        copy.start()
+    for load, store in zip(loads, stores):
+        load.wait()
+        store.start()
+    for copy in stores:
+        copy.wait()
+
+
 def shards(
     prompt_q, prompt_kv, prefix_length, decode_q, decode_kv, fresh_kv, source_prompt, cache_length
 ):
@@ -396,7 +415,7 @@
     q = q.reshape(SEQ, KVH, ROWS, HD)
     fresh = fresh_kv[0].reshape(SEQ, 2, STEPS, KVH, HD).transpose(0, 1, 3, 2, 4)
     fresh = fresh.reshape(SEQ, 2, KVH * STEPS, HD)
-    src = jnp.pad(source_prompt[0, :, 0][None, :], ((0, 0), (0, 128 - SEQ)))
+    src = source_prompt[0, :, 0][None, :]
     vmem = pl.BlockSpec(memory_space=VMEM)
     smem = pl.BlockSpec(memory_space=pltpu.SMEM)
     anys = pl.BlockSpec(memory_space=pl.ANY)
@@ -416,12 +435,12 @@
             VMEM((SLOTS, NZH, KEYS, HD), BF16),
             VMEM((SLOTS, NZH, KEYS + 16, HD), BF16),
             VMEM((RING, SEQ, ROWS, HD), BF16),
-            VMEM((RING, 1, 128), jnp.int32),
-            pltpu.SMEM((RING, 1, 128), jnp.int32),
+            VMEM((RING, 1, SEQ), jnp.int32),
+            pltpu.SMEM((RING, 1, SEQ), jnp.int32),
             VMEM((RING, SEQ, ROWS, HD), BF16),
-            VMEM((RING, ROWS, 128), F32),
+            VMEM((RING, 8, 128), F32),
             VMEM((RING, SEQ, ROWS, HD), BF16),
-            VMEM((RING, ROWS, 128), F32),
+            VMEM((RING, 8, 128), F32),
             VMEM((SEQ, KVH * ROWS, HD), F32),
             VMEM((KVH * ROWS, 128), F32),
             VMEM((1, C, 2 * PER_KV * HD), BF16),
@@ -442,6 +461,19 @@
         ),
         name="attention",
     )(prefix_length, cache_length[0], prompt_q, prompt_kv, q, decode_kv[0], fresh, src)
+    prompt_out, out = pl.pallas_call(
+        copy_kernel,
+        out_shape=(shape(prompt_out.shape, BF16), shape(out.shape, BF16)),
+        in_specs=[anys] * 2,
+        out_specs=[anys] * 2,
+        scratch_shapes=[
+            VMEM(prompt_out.shape, BF16),
+            VMEM(out.shape, BF16),
+            sem((PARTS + 1,)),
+            sem((PARTS + 1,)),
+        ],
+        name="place",
+    )(prompt_out, out)
     out = out.reshape(SEQ, HEADS, STEPS, HD).transpose(0, 2, 1, 3)
     return prompt_out, out.reshape(1, SEQ, STEPS, HEADS * HD)
 

time: 83.6 us -> 78.8 us (0.943)
  local copies, waits for them, and re-layouts: 6.28 us -> 0 us
  Pallas kernels: 75.8 us -> 77.4 us
    unnamed x2 -> x0, local copies, waits for them, and re-layouts: 5.11 us -> none
    pallas_call x0 -> x1, Pallas kernels: none -> 2.08 us  [shards(): pl.pallas_call(copy_kernel, out_shape=(shape(prompt_out.shape, BF16), sha...]
    pad x1 -> x0, local copies, waits for them, and re-layouts: 1.17 us -> none  [shards(): src = jnp.pad(source_prompt[0, :, 0][None, :], ((0, 0), (0, 128 - SEQ)))]
where the time goes in v3:
time: 78.8 us; the launch traced here: 78.7 us
  Pallas kernels  77.4 us (98%)
  between operations  1.29 us (2%)
    pallas_call x1, Pallas kernels, shards(): pl.pallas_call(kernel, out_shape=(shape((1, C, 2 * PER_KV * HD), BF16), s...  75.3 us
    pallas_call x1, Pallas kernels, shards(): pl.pallas_call(copy_kernel, out_shape=(shape(prompt_out.shape, BF16), sha...  2.08 us

profile of v3, /device:TPU:1, one launch (start us, length us, event | category | flops | bytes accessed | tf_op | source)
XLA Modules:
  0.0 78.7 jit_solution(14698419916560534467)
XLA Ops:
  1.3 75.3 %attention.1 = (bf16[1,64,2048]{2,1,0:T(8,128)(2,1)}, bf16[32,8,16,128]{3,2,1,0:T(8,128)(2,1)}) custom-call(s32[1]{0:T(128)S(6)} %copy.13.plen, s32[32]{0:T(128)} %bitcast.21, bf16[1,64,2048]{2,1,0:T(8,128)(2,1)} %prompt_q_hbm.1, bf16[1,2,192,256]{3,2,1,0:T(8,128)(2,1)} %kv.1, bf16[32,8,16,128]{3,2,1,0:T(8,128)(2,1)} %bitcast.19, ...), custom_call_target="tpu_custom_call" | custom-call | tf_op jit(solution)/shard_map/attention/pallas_call | solution.py:424
  76.6 2.1 %place.1 = (bf16[1,64,2048]{2,1,0:T(8,128)(2,1)}, bf16[32,8,16,128]{3,2,1,0:T(8,128)(2,1)}) custom-call(bf16[1,64,2048]{2,1,0:T(8,128)(2,1)} %get-tuple-element.6.a, bf16[32,8,16,128]{3,2,1,0:T(8,128)(2,1)} %get-tuple-element.7.b), custom_call_target="tpu_custom_call" | custom-call | tf_op jit(solution)/shard_map/place/pallas_call | solution.py:464

commit v4 on v3

--- a/solution.py
+++ b/solution.py
@@ -201,13 +201,14 @@
 
 def kernel(
     plen, lengths, prompt_q_hbm, kv, q, cache_hbm, fresh_hbm, src, prompt_out, out,
-    blk_a, blk_b, ka, kb, qg, srcg, sources, ro, rs, bo, bs, acc, stats,
+    blk_a, blk_b, ka, kb, ka2, kb2, qg, srcg, sources, ro, rs, bo, bs, acc, stats,
     prompt_q, q_own, cache, fresh, load, local,
     send_q, recv_q, send_s, recv_s, send_f, recv_f, send_1, recv_1, send_2, recv_2, send_c, recv_c,
     send_o, recv_o, send_t, recv_t,
 ):
     x, y, zh, core, zl = position()
     ring = zh * NZL + zl
+    opposite = lax.rem(ring + RING // 2, RING)
     sibling = device(x, y, zh, 1 - core, zl)
     ring_peers = [ring_device(x, y, core, lax.rem(ring + d, RING)) for d in range(1, RING)]
     x_peers = [device(lax.rem(x + d, NX), y, zh, core, zl) for d in range(1, NX)]
@@ -230,37 +231,189 @@
         pltpu.make_async_copy(cache_hbm, cache, load.at[6]),
         pltpu.make_async_copy(fresh_hbm, fresh, load.at[7]),
     ]
-    for copy in blocks:
+    local_copies = [
+        pltpu.make_async_copy(q.at[:, ring_head(ring)], qg.at[ring], local.at[0]),
+        pltpu.make_async_copy(q.at[:, ring_head(opposite)], qg.at[opposite], local.at[1]),
+        pltpu.make_async_copy(src, srcg.at[ring], local.at[2]),
+    ]
+    for copy in blocks + loads + local_copies:
         copy.start()
     row_bias = jnp.where(
         lax.broadcasted_iota(jnp.int32, (16, PRE), 1) < plen[0], 0.0, NEGATIVE
     ).astype(BF16)
     for half in range(2):
         blk_b[half, KEYS:] = row_bias
-    enter(ring_peers + x_peers + y_peers + [sibling])
     for copy in blocks:
         copy.wait()
-
     mine = slot_of(x, y, core)
+    ka[mine, zh] = blk_a[zh]
+    kb[mine, zh] = blk_b[zh]
+    ka2[mine, zh] = blk_a[1 - zh]
+    kb2[mine, zh] = blk_b[1 - zh]
+    enter(ring_peers + x_peers + y_peers + [sibling])
+
     antipode = ring_peers[RING // 2 - 1]
     far_copies = [
-        remote(blk.at[1 - zh], dst.at[mine, zh], send_f.at[i], recv_f.at[i], antipode)
-        for i, (blk, dst) in enumerate(((blk_a, ka), (blk_b, kb)))
+        remote(blk.at[head], dst.at[mine, zh], send_f.at[i], recv_f.at[i], antipode)
+        for i, (blk, dst, head) in enumerate(
+            ((blk_a, ka, 1 - zh), (blk_b, kb, 1 - zh), (blk_a, ka2, zh), (blk_b, kb2, zh))
+        )
     ]
-    for copy in far_copies:
+    for copy in far_copies[:2]:
         copy.start()
-    local_copies = [
-        pltpu.make_async_copy(blk_a.at[zh], ka.at[mine, zh], local.at[0]),
-        pltpu.make_async_copy(blk_b.at[zh], kb.at[mine, zh], local.at[1]),
-        pltpu.make_async_copy(q.at[:, ring_head(ring)], qg.at[ring], local.at[2]),
-        pltpu.make_async_copy(src, srcg.at[ring], local.at[3]),
-    ]
-    for copy in local_copies:
-        copy.start()
+
+    def slot_at(path, first, second):
+        dx, dy = (first, second) if path == 0 else (second, first)
+        return slot_of(lax.rem(x + NX - dx, NX), lax.rem(y + NY - dy, NY), core)
+
+    def along(path, phase, d):
+        return (x_peers if (path + phase) % 2 == 0 else y_peers)[d - 1]
+
+    streams = (
+        (lambda slot: (ka.at[slot, zh], kb.at[slot, zh])),
+        (lambda slot: (ka.at[slot, 1 - zh], kb.at[slot, 1 - zh])),
+        (lambda slot: (ka2.at[slot], kb2.at[slot])),
+    )
+    pieces = ((), (), ((0, 1), (1, 3)))
+
+    def part(stream, path, slot, piece):
+        ref = streams[stream](slot)[path]
+        return ref if piece is None else ref.at[piece]
+
+    def first_copies(stream, path, way):
+        if way != 2 or not pieces[stream]:
+            ref = part(stream, path, mine, None)
+            return [
+                remote(
+                    ref, ref, send_1.at[stream, path, way], recv_1.at[stream, path, way],
+                    along(path, 0, way),
+                )
+            ]
+        copies = []
+        for piece, to in pieces[stream]:
+            ref = part(stream, path, slot_at(path, to, 0), piece)
+            i = 0 if to == 1 else 2
+            copies.append(
+                remote(
+                    ref, ref, send_1.at[stream, path, i], recv_1.at[stream, path, i],
+                    along(path, 0, to),
+                )
+            )
+        return copies
+
+    def second_copies(stream, path, d, way):
+        if way != 2 or not pieces[stream]:
+            ref = part(stream, path, slot_at(path, d, 0), None)
+            return [
+                remote(
+                    ref, ref, send_2.at[stream, path, d, way], recv_2.at[stream, path, d, way],
+                    along(path, 1, way),
+                )
+            ]
+        copies = []
+        for piece, to in pieces[stream]:
+            ref = part(stream, path, slot_at(path, d, to), piece)
+            i = 0 if to == 1 else 2
+            copies.append(
+                remote(
+                    ref, ref, send_2.at[stream, path, d, i], recv_2.at[stream, path, d, i],
+                    along(path, 1, to),
+                )
+            )
+        return copies
+
+    def side_copies(stream, path, d, e):
+        ref = part(stream, path, slot_at(path, d, e), None)
+        return [
+            remote(
+                ref, ref, send_c.at[stream, path, d, e], recv_c.at[stream, path, d, e], sibling
+            )
+        ]
+
+    def start(copies):
+        for copy in copies:
+            copy.start()
+
+    def arrived(copies):
+        for copy in copies:
+            copy.wait_recv()
+
+    def gone(copies):
+        for copy in copies:
+            copy.wait_send()
+
+    def begin(stream):
+        for path in range(2):
+            start(first_copies(stream, path, 1))
+            start(first_copies(stream, path, 3))
+            if not pieces[stream]:
+                start(first_copies(stream, path, 2))
+
+    def go_on(stream):
+        if not pieces[stream]:
+            return
+        for path in range(2):
+            for piece, to in pieces[stream]:
+                arrived(first_copies(stream, path, to))
+            start(first_copies(stream, path, 2))
+
+    def spread(stream, d):
+        passed = [to for piece, to in pieces[stream]]
+        for path in range(2):
+            if d > 0 and d not in passed:
+                arrived(first_copies(stream, path, d))
+            start(second_copies(stream, path, d, 1))
+            start(second_copies(stream, path, d, 3))
+            if not pieces[stream]:
+                start(second_copies(stream, path, d, 2))
+            start(side_copies(stream, path, d, 0))
+
+    def go_on_second(stream, d):
+        if not pieces[stream]:
+            return
+        for path in range(2):
+            for piece, to in pieces[stream]:
+                arrived(second_copies(stream, path, d, to))
+            start(second_copies(stream, path, d, 2))
+            for piece, to in pieces[stream]:
+                start(side_copies(stream, path, d, to))
+
+    def finish(stream, d):
+        passed = [to for piece, to in pieces[stream]]
+        for path in range(2):
+            for way in (1, 3, 2):
+                if way not in passed:
+                    arrived(second_copies(stream, path, d, way))
+                    start(side_copies(stream, path, d, way))
+
+    def sides(stream):
+        return [
+            copy
+            for path in range(2)
+            for d in range(4)
+            for e in range(4)
+            for copy in side_copies(stream, path, d, e)
+        ]
+
+    def spreading(stream):
+        copies = []
+        for path in range(2):
+            for way in (1, 3, 2):
+                copies += first_copies(stream, path, way)
+                for d in range(4):
+                    copies += second_copies(stream, path, d, way)
+        return copies
+
+    def local_rows(first, last):
+        local_part(first, last, lengths, q_own, cache, fresh, acc, stats)
+
+    begin(0)
+    spread(0, 0)
     q_copies = []
-    for d in (4, 3, 5, 2, 6, 1, 7):
+    src_copies = []
+    for d in (3, 5, 2, 6, 1, 7):
         other = lax.rem(ring + d, RING)
-        q_copies.append(
+        src_copies.append(
             remote(src, srcg.at[ring], send_s.at[d - 1], recv_s.at[d - 1], ring_peers[d - 1])
         )
         q_copies.append(
@@ -272,74 +425,57 @@
                 ring_peers[d - 1],
             )
         )
-    for copy in q_copies:
-        copy.start()
-    for copy in loads:
-        copy.start()
-
+    start(far_copies[2:])
+    start(src_copies + q_copies)
+    go_on(0)
+    spread(0, 1)
+    spread(0, 3)
     loads[0].wait()
     prefill_part(0, plen, prompt_q, blk_a, blk_b, prompt_out)
-    local_copies[0].wait()
-    local_copies[1].wait()
-    for copy in far_copies:
-        copy.wait_recv()
-
-    paths = ((ka, x_peers, y_peers), (kb, y_peers, x_peers))
-
-    def slot_at(path, first, second):
-        if path == 0:
-            return slot_of(lax.rem(x + NX - first, NX), lax.rem(y + NY - second, NY), core)
-        return slot_of(lax.rem(x + NX - second, NX), lax.rem(y + NY - first, NY), core)
-
-    sent = []
-
-    def push(ref, slot, send, recv, peer):
-        copy = remote(ref.at[slot], ref.at[slot], send, recv, peer)
-        copy.start()
-        sent.append(copy)
-
-    firsts = [[], []]
-    seconds = [[], []]
-    sides = []
-    for path, (ref, first_peers, second_peers) in enumerate(paths):
-        for d in range(1, 4):
-            push(ref, mine, send_1.at[path, d - 1], recv_1.at[path, d - 1], first_peers[d - 1])
-            firsts[path].append(sent[-1])
-    for d in range(4):
-        for path, (ref, first_peers, second_peers) in enumerate(paths):
-            if d > 0:
-                firsts[path][d - 1].wait_recv()
-            slot = slot_at(path, d, 0)
-            for e in range(1, 4):
-                push(
-                    ref, slot, send_2.at[path, d, e - 1], recv_2.at[path, d, e - 1],
-                    second_peers[e - 1],
-                )
-                seconds[path].append(sent[-1])
-            push(ref, slot, send_c.at[path, d, 0], recv_c.at[path, d, 0], sibling)
-            sides.append(sent[-1])
-        if d == 0:
-            prefill_part(1, plen, prompt_q, blk_a, blk_b, prompt_out)
+    spread(0, 2)
+    arrived(far_copies[:2])
+    begin(1)
+    spread(1, 0)
+    go_on_second(0, 0)
     for copy in loads[1:]:
         copy.wait()
-    for d in range(4):
-        local_part(d * 8, d * 8 + 8, lengths, q_own, cache, fresh, acc, stats)
-        for path, (ref, first_peers, second_peers) in enumerate(paths):
-            for e in range(1, 4):
-                seconds[path][d * 3 + e - 1].wait_recv()
-                push(
-                    ref, slot_at(path, d, e), send_c.at[path, d, e], recv_c.at[path, d, e], sibling
-                )
-                sides.append(sent[-1])
-    for copy in q_copies:
-        copy.wait_recv()
-    local_copies[2].wait()
-    local_copies[3].wait()
-    place = pltpu.make_async_copy(srcg, sources, local.at[4])
+    prefill_part(1, plen, prompt_q, blk_a, blk_b, prompt_out)
+    go_on(1)
+    spread(1, 1)
+    spread(1, 3)
+    go_on_second(0, 1)
+    go_on_second(0, 3)
+    spread(1, 2)
+    arrived(far_copies[2:])
+    begin(2)
+    spread(2, 0)
+    local_rows(0, 4)
+    go_on_second(1, 0)
+    go_on_second(0, 2)
+    local_rows(4, 8)
+    go_on_second(1, 1)
+    go_on_second(1, 3)
+    local_rows(8, 12)
+    go_on_second(1, 2)
+    local_rows(12, 16)
+    for d in (0, 1, 3, 2):
+        finish(0, d)
+    local_rows(16, 24)
+    arrived(src_copies)
+    for copy in local_copies:
+        copy.wait()
+    srcg[opposite] = srcg[ring]
+    place = pltpu.make_async_copy(srcg, sources, local.at[3])
     place.start()
+    local_rows(24, 32)
     place.wait()
-    for copy in sides:
-        copy.wait_recv()
+    for d in (0, 1, 3, 2):
+        finish(1, d)
+    go_on(2)
+    spread(2, 1)
+    spread(2, 3)
+    arrived(q_copies)
+    arrived(sides(0) + sides(1))
 
     def answers(d):
         other = lax.rem(ring + d, RING)
@@ -355,41 +491,56 @@
         ]
 
     def distance(k):
-        return RING // 2 + (1 - 2 * lax.rem(k, 2)) * ((k + 1) // 2)
+        return RING // 2 + (2 * lax.rem(k, 2) - 1) * (1 + k // 2)
 
     def answer(k, carry):
         d = distance(k)
         remote_part(lax.rem(ring + d, RING), sources, ka, kb, qg, ro, rs)
 
-        @pl.when(k < RING - 1)
+        @pl.when(k < RING - 2)
         def _():
-            for copy in answers(d):
-                copy.start()
+            start(answers(d))
+
+        @pl.when(k == 0)
+        def _():
+            spread(2, 2)
+
+        @pl.when(k == 1)
+        def _():
+            go_on_second(2, 0)
+
+        @pl.when(k == 3)
+        def _():
+            go_on_second(2, 1)
+            go_on_second(2, 3)
+
+        @pl.when(k == 4)
+        def _():
+            go_on_second(2, 2)
 
         return carry
-
-    lax.fori_loop(0, RING, answer, 0)
-    bo[ring] = ro[ring]
-    bs[ring] = rs[ring]
 
     def merge(k, carry):
         d = distance(k)
-
-        @pl.when(k < RING - 1)
-        def _():
-            for copy in answers(d):
-                copy.wait()
-
+        for copy in answers(d):
+            copy.wait()
         merge_part(lax.rem(ring + RING - d, RING), bo, bs, acc, stats, out)
         return carry
 
-    lax.fori_loop(0, RING, merge, 0)
-    for copy in q_copies:
-        copy.wait_send()
-    for copy in far_copies:
-        copy.wait_send()
-    for copy in sent:
-        copy.wait_send()
+    lax.fori_loop(0, RING - 1, answer, 0)
+    for d in (0, 1, 3, 2):
+        finish(2, d)
+    lax.fori_loop(0, 2, merge, 0)
+    arrived(sides(2))
+    remote_part(opposite, sources, ka2, kb2, qg, ro, rs)
+    for place_at in (ring, opposite):
+        bo[place_at] = ro[place_at]
+        bs[place_at] = rs[place_at]
+        merge_part(place_at, bo, bs, acc, stats, out)
+    lax.fori_loop(2, RING - 2, merge, 0)
+    gone(q_copies + src_copies + far_copies)
+    for stream in range(3):
+        gone(spreading(stream) + sides(stream))
 
 
 def copy_kernel(a, b, out_a, out_b, stage_a, stage_b, sem_in, sem_out):
@@ -434,6 +585,8 @@
             VMEM((2, KEYS + 16, HD), BF16),
             VMEM((SLOTS, NZH, KEYS, HD), BF16),
             VMEM((SLOTS, NZH, KEYS + 16, HD), BF16),
+            VMEM((SLOTS, NZH, KEYS, HD), BF16),
+            VMEM((SLOTS, NZH, KEYS + 16, HD), BF16),
             VMEM((RING, SEQ, ROWS, HD), BF16),
             VMEM((RING, 1, SEQ), jnp.int32),
             pltpu.SMEM((RING, 1, SEQ), jnp.int32),
@@ -448,13 +601,13 @@
             VMEM((SEQ, 2, LOC, KVH * HD), BF16),
             VMEM((SEQ, 2, KVH * STEPS, HD), BF16),
             sem((8,)),
-            sem((5,)),
+            sem((4,)),
         ]
         + [sem((RING - 1,))] * 4
-        + [sem((2,))] * 2
-        + [sem((2, 3))] * 2
-        + [sem((2, 4, 3))] * 2
-        + [sem((2, 4, 4))] * 2
+        + [sem((4,))] * 2
+        + [sem((3, 2, 4))] * 2
+        + [sem((3, 2, 4, 4))] * 2
+        + [sem((3, 2, 4, 4))] * 2
         + [sem((RING,))] * 4,
         compiler_params=pltpu.CompilerParams(
             collective_id=0, has_side_effects=True, vmem_limit_bytes=58 * MIB

time: 78.8 us -> 71.2 us (0.904)
  Pallas kernels: 77.4 us -> 69.8 us
    pallas_call x1, Pallas kernels: 75.3 us -> 67.7 us  [shards(): pl.pallas_call(kernel, out_shape=(shape((1, C, 2 * PER_KV * HD), BF16), s...]
where the time goes in v4:
time: 71.2 us; the launch traced here: 71.1 us
  Pallas kernels  69.8 us (98%)
  between operations  1.29 us (2%)
    pallas_call x1, Pallas kernels, shards(): pl.pallas_call(kernel, out_shape=(shape((1, C, 2 * PER_KV * HD), BF16), s...  67.7 us
    pallas_call x1, Pallas kernels, shards(): pl.pallas_call(copy_kernel, out_shape=(shape(prompt_out.shape, BF16), sha...  2.08 us

profile of v4, /device:TPU:1, one launch (start us, length us, event | category | flops | bytes accessed | tf_op | source)
XLA Modules:
  0.0 71.1 jit_solution(16613064130390251838)
XLA Ops:
  1.3 67.7 %attention.1 = (bf16[1,64,2048]{2,1,0:T(8,128)(2,1)}, bf16[32,8,16,128]{3,2,1,0:T(8,128)(2,1)}) custom-call(s32[1]{0:T(128)S(6)} %copy.13.plen, s32[32]{0:T(128)} %bitcast.21, bf16[1,64,2048]{2,1,0:T(8,128)(2,1)} %prompt_q_hbm.1, bf16[1,2,192,256]{3,2,1,0:T(8,128)(2,1)} %kv.1, bf16[32,8,16,128]{3,2,1,0:T(8,128)(2,1)} %bitcast.19, ...), custom_call_target="tpu_custom_call" | custom-call | tf_op jit(solution)/shard_map/attention/pallas_call | solution.py:575
  69.0 2.1 %place.1 = (bf16[1,64,2048]{2,1,0:T(8,128)(2,1)}, bf16[32,8,16,128]{3,2,1,0:T(8,128)(2,1)}) custom-call(bf16[1,64,2048]{2,1,0:T(8,128)(2,1)} %get-tuple-element.6.a, bf16[32,8,16,128]{3,2,1,0:T(8,128)(2,1)} %get-tuple-element.7.b), custom_call_target="tpu_custom_call" | custom-call | tf_op jit(solution)/shard_map/place/pallas_call | solution.py:617

commit v5 on v4

--- a/solution.py
+++ b/solution.py
@@ -143,7 +143,7 @@
 
 def remote_part(ring, sources, ka, kb, qg, ro, rs):
     lane = lax.broadcasted_iota(jnp.int32, (ROWS, 128), 1)
-    group = 16
+    group = 32
 
     def body(block, table):
         seqs = [block * group + i for i in range(group)]

time: 71.2 us -> 70.3 us (0.987)
  Pallas kernels: 69.8 us -> 68.9 us
    pallas_call x1, Pallas kernels: 67.7 us -> 66.8 us  [shards(): pl.pallas_call(kernel, out_shape=(shape((1, C, 2 * PER_KV * HD), BF16), s...]
where the time goes in v5:
time: 70.3 us; the launch traced here: 70.2 us
  Pallas kernels  68.9 us (98%)
  between operations  1.29 us (2%)
    pallas_call x1, Pallas kernels, shards(): pl.pallas_call(kernel, out_shape=(shape((1, C, 2 * PER_KV * HD), BF16), s...  66.8 us
    pallas_call x1, Pallas kernels, shards(): pl.pallas_call(copy_kernel, out_shape=(shape(prompt_out.shape, BF16), sha...  2.08 us

profile of v5, /device:TPU:1, one launch (start us, length us, event | category | flops | bytes accessed | tf_op | source)
XLA Modules:
  0.0 70.2 jit_solution(3703542498401196946)
XLA Ops:
  1.3 66.8 %attention.1 = (bf16[1,64,2048]{2,1,0:T(8,128)(2,1)}, bf16[32,8,16,128]{3,2,1,0:T(8,128)(2,1)}) custom-call(s32[1]{0:T(128)S(6)} %copy.13.plen, s32[32]{0:T(128)} %bitcast.21, bf16[1,64,2048]{2,1,0:T(8,128)(2,1)} %prompt_q_hbm.1, bf16[1,2,192,256]{3,2,1,0:T(8,128)(2,1)} %kv.1, bf16[32,8,16,128]{3,2,1,0:T(8,128)(2,1)} %bitcast.19, ...), custom_call_target="tpu_custom_call" | custom-call | tf_op jit(solution)/shard_map/attention/pallas_call | solution.py:575
  68.1 2.1 %place.1 = (bf16[1,64,2048]{2,1,0:T(8,128)(2,1)}, bf16[32,8,16,128]{3,2,1,0:T(8,128)(2,1)}) custom-call(bf16[1,64,2048]{2,1,0:T(8,128)(2,1)} %get-tuple-element.6.a, bf16[32,8,16,128]{3,2,1,0:T(8,128)(2,1)} %get-tuple-element.7.b), custom_call_target="tpu_custom_call" | custom-call | tf_op jit(solution)/shard_map/place/pallas_call | solution.py:617

commit v6 on v5

--- a/solution.py
+++ b/solution.py
@@ -530,13 +530,15 @@
     lax.fori_loop(0, RING - 1, answer, 0)
     for d in (0, 1, 3, 2):
         finish(2, d)
+    bo[ring] = ro[ring]
+    bs[ring] = rs[ring]
+    merge_part(ring, bo, bs, acc, stats, out)
     lax.fori_loop(0, 2, merge, 0)
     arrived(sides(2))
     remote_part(opposite, sources, ka2, kb2, qg, ro, rs)
-    for place_at in (ring, opposite):
-        bo[place_at] = ro[place_at]
-        bs[place_at] = rs[place_at]
-        merge_part(place_at, bo, bs, acc, stats, out)
+    bo[opposite] = ro[opposite]
+    bs[opposite] = rs[opposite]
+    merge_part(opposite, bo, bs, acc, stats, out)
     lax.fori_loop(2, RING - 2, merge, 0)
     gone(q_copies + src_copies + far_copies)
     for stream in range(3):

time: 70.3 us -> 70.3 us (level)
  no operation moved by 1% of the time
where the time goes in v6:
time: 70.3 us; the launch traced here: 70.2 us
  Pallas kernels  68.9 us (98%)
  between operations  1.29 us (2%)
    pallas_call x1, Pallas kernels, shards(): pl.pallas_call(kernel, out_shape=(shape((1, C, 2 * PER_KV * HD), BF16), s...  66.8 us
    pallas_call x1, Pallas kernels, shards(): pl.pallas_call(copy_kernel, out_shape=(shape(prompt_out.shape, BF16), sha...  2.08 us

profile of v6, /device:TPU:1, one launch (start us, length us, event | category | flops | bytes accessed | tf_op | source)
XLA Modules:
  0.0 70.2 jit_solution(2921182735180720058)
XLA Ops:
  1.3 66.8 %attention.1 = (bf16[1,64,2048]{2,1,0:T(8,128)(2,1)}, bf16[32,8,16,128]{3,2,1,0:T(8,128)(2,1)}) custom-call(s32[1]{0:T(128)S(6)} %copy.13.plen, s32[32]{0:T(128)} %bitcast.21, bf16[1,64,2048]{2,1,0:T(8,128)(2,1)} %prompt_q_hbm.1, bf16[1,2,192,256]{3,2,1,0:T(8,128)(2,1)} %kv.1, bf16[32,8,16,128]{3,2,1,0:T(8,128)(2,1)} %bitcast.19, ...), custom_call_target="tpu_custom_call" | custom-call | tf_op jit(solution)/shard_map/attention/pallas_call | solution.py:577
  68.1 2.1 %place.1 = (bf16[1,64,2048]{2,1,0:T(8,128)(2,1)}, bf16[32,8,16,128]{3,2,1,0:T(8,128)(2,1)}) custom-call(bf16[1,64,2048]{2,1,0:T(8,128)(2,1)} %get-tuple-element.6.a, bf16[32,8,16,128]{3,2,1,0:T(8,128)(2,1)} %get-tuple-element.7.b), custom_call_target="tpu_custom_call" | custom-call | tf_op jit(solution)/shard_map/place/pallas_call | solution.py:619
